TPU v7x, 128 devices: a whole 4x4x4 slice. The times are simulated.
128 devices in a mesh: dp: 8 (over y, core), expert: 16 (over x, z).
Axes of the slice: x: 4, y: 4, z: 4, core: 2. Of those that a mesh axis runs over, the one named last changes fastest.
Arguments:
- tokens: bfloat16 [4096, 4096], P('expert', 'dp'), may hold values from -6 to 6
- expert_ids: int32 [4096, 8], P('expert'), may hold values from 0 to 63, all different within a row; in each aligned block of 256 rows (0 to 255, 256 to 511, ...) at most 48 rows name the same one
- route_weights: float32 [4096, 8], P('expert'), may hold values from 0.05 to 1
- w_gate: bfloat16 [64, 4096, 768], P('expert', 'dp'), may hold values from -0.09375 to 0.09375
- w_up: bfloat16 [64, 4096, 768], P('expert', 'dp'), may hold values from -0.09375 to 0.09375
- w_down: bfloat16 [64, 768, 4096], P('expert', None, 'dp'), may hold values from -0.21875 to 0.21875
- out_grad: bfloat16 [4096, 4096], P('expert', 'dp'), may hold values from -6 to 6
Outputs:
- mixed: bfloat16 [4096, 4096], P('expert', 'dp')
- grad_tokens: bfloat16 [4096, 4096], P('expert', 'dp')
- grad_route: float32 [4096, 8], P('expert')
- grad_gate: bfloat16 [64, 4096, 768], P('expert', 'dp')
- grad_up: bfloat16 [64, 4096, 768], P('expert', 'dp')
- grad_down: bfloat16 [64, 768, 4096], P('expert', None, 'dp')
Inputs may be any that keep to these rules, and one draw needn't show every extreme that they name: `expert_ids`: each token names 8 different experts; within the 256 tokens of one index of the expert axis no expert is named more than 48 times, a bound that some block reaches.
All inputs are finite; a program needn't handle non-finite values.
Results may differ from a plain program's by a relative error of at most 0.033.
Values may be sent and summed in bfloat16 or wider, within the bound.
A program may use at most 128 MiB of HBM per device.

v0:
```python
import jax
import jax.numpy as jnp
from jax import lax
from jax.sharding import PartitionSpec as P


def activate(gate_up, hidden):
    gate = gate_up[..., :hidden]
    up = gate_up[..., hidden:]
    return (jax.nn.silu(gate) * up).astype(jnp.bfloat16)


def derive(gate_up, grad_hidden, hidden):
    gate = gate_up[..., :hidden]
    up = gate_up[..., hidden:]
    sig = jax.nn.sigmoid(gate)
    d_gate = grad_hidden * up * sig * (1.0 + gate * (1.0 - sig))
    d_up = grad_hidden * jax.nn.silu(gate)
    return jnp.concatenate((d_gate.astype(jnp.bfloat16), d_up.astype(jnp.bfloat16)), -1)


def local(tokens, expert_ids, route_weights, w_gate, w_up, w_down, out_grad):
    tok_count, top_count = expert_ids.shape
    exp_local, width_part, hidden = w_gate.shape
    owners = lax.axis_size("expert")
    experts = exp_local * owners
    capacity = 3 * tok_count * top_count // (2 * experts)
    table = jnp.arange(experts, dtype=jnp.int32)
    member = (expert_ids[:, :, None] == table).astype(jnp.int32)
    counts = jnp.sum(member, 1)
    before = jnp.cumsum(counts, 0) - counts
    rank = jnp.sum(member * before[:, None, :], 2)
    slot = expert_ids * capacity + rank
    spread = jnp.broadcast_to(tokens[:, None, :], (tok_count, top_count, width_part))
    sent_rows = jnp.zeros((experts * capacity, width_part), jnp.bfloat16).at[slot].set(spread)
    scaled = (route_weights[:, :, None] * out_grad[:, None, :].astype(jnp.float32)).astype(
        jnp.bfloat16
    )
    sent_grads = jnp.zeros((experts * capacity, width_part), jnp.bfloat16).at[slot].set(scaled)
    layout = (owners, exp_local, capacity, width_part)
    recv_rows, recv_grads = (
        lax.all_to_all(
            sent_rows.reshape(layout), "expert", split_axis=0, concat_axis=2, tiled=True
        ),
        lax.all_to_all(
            sent_grads.reshape(layout), "expert", split_axis=0, concat_axis=2, tiled=True
        ),
    )
    recv_rows = recv_rows[0]
    recv_grads = recv_grads[0]
    partial_value = jnp.concatenate(
        (
            jnp.einsum("erd,edf->erf", recv_rows, w_gate, preferred_element_type=jnp.float32),
            jnp.einsum("erd,edf->erf", recv_rows, w_up, preferred_element_type=jnp.float32),
        ),
        -1,
    )
    gate_up = lax.psum(partial_value.astype(jnp.bfloat16), "dp").astype(jnp.float32)
    hidden_act = activate(gate_up, hidden)
    expert_out = jnp.einsum(
        "erf,efd->erd", hidden_act, w_down, preferred_element_type=jnp.float32
    ).astype(jnp.bfloat16)
    returned = lax.all_to_all(
        expert_out, "expert", split_axis=1, concat_axis=0, tiled=True
    ).reshape(experts * capacity, width_part)
    picked = returned[slot].astype(jnp.float32)
    mixed = jnp.einsum("tk,tkd->td", route_weights, picked).astype(jnp.bfloat16)
    router_part = jnp.einsum("td,tkd->tk", out_grad.astype(jnp.float32), picked)
    grad_down = jnp.einsum(
        "erf,erd->efd", hidden_act, recv_grads, preferred_element_type=jnp.float32
    ).astype(jnp.bfloat16)
    hidden_part = jnp.einsum("erd,efd->erf", recv_grads, w_down, preferred_element_type=jnp.float32)
    grad_hidden, grad_route = (
        lax.psum(hidden_part.astype(jnp.bfloat16), "dp").astype(jnp.float32),
        lax.psum(router_part.astype(jnp.bfloat16), "dp").astype(jnp.float32),
    )
    grad_gate_up = derive(gate_up, grad_hidden, hidden)
    d_gate = grad_gate_up[..., :hidden]
    d_up = grad_gate_up[..., hidden:]
    grad_gate = jnp.einsum(
        "erd,erf->edf", recv_rows, d_gate, preferred_element_type=jnp.float32
    ).astype(jnp.bfloat16)
    grad_up = jnp.einsum(
        "erd,erf->edf", recv_rows, d_up, preferred_element_type=jnp.float32
    ).astype(jnp.bfloat16)
    slot_grad_out = (
        jnp.einsum("erf,edf->erd", d_gate, w_gate, preferred_element_type=jnp.float32)
        + jnp.einsum("erf,edf->erd", d_up, w_up, preferred_element_type=jnp.float32)
    ).astype(jnp.bfloat16)
    back = lax.all_to_all(slot_grad_out, "expert", split_axis=1, concat_axis=0, tiled=True).reshape(
        experts * capacity, width_part
    )
    grad_tokens = jnp.sum(back[slot].astype(jnp.float32), 1).astype(jnp.bfloat16)
    return (mixed, grad_tokens, grad_route, grad_gate, grad_up, grad_down)


def solution(mesh):
    in_specs = (
        P("expert", "dp"),
        P("expert", None),
        P("expert", None),
        P("expert", "dp", None),
        P("expert", "dp", None),
        P("expert", None, "dp"),
        P("expert", "dp"),
    )
    out_specs = (
        P("expert", "dp"),
        P("expert", "dp"),
        P("expert", None),
        P("expert", "dp", None),
        P("expert", "dp", None),
        P("expert", None, "dp"),
    )
    return jax.shard_map(local, mesh=mesh, in_specs=in_specs, out_specs=out_specs, check_vma=False)
```

profile of v0, /device:TPU:0, one launch (start us, length us, event | category | flops | bytes accessed | tf_op | source)
XLA Modules:
  0.0 474.0 jit_solution(2898269864645621025)
XLA Ops:
  7.2 0.0 copy-start
  7.2 0.9 convert_reduce_fusion
  8.1 0.6 reduce-window.6
  8.7 0.2 slice_reduce_fusion
  8.9 0.1 fusion.20
  9.0 0.8 select_reduce_fusion
  9.8 0.7 compare_select_fusion
  10.5 0.1 copy.71
  10.7 0.1 reshape.68
  10.8 0.0 copy-start.14
  10.8 11.9 %scatter_custom_fusion = bf16[3072,512]{1,0:T(8,128)(2,1)} fusion(s32[2048]{0:T(1024)S(1)} %reshape.68, bf16[]{:T(256)} %constant.6.clone.1, bf16[256,512]{1,0:T(8,128)(2,1)} %param.7), kind=kCustom, calls=%fused_computation.30 | custom fusion | bytes 3407874 | tf_op jit(solution)/shard_map/scatter | solution.py:35
  22.7 8.1 %all-to-all-start = ((bf16[16,4,48,512]{3,2,1,0:T(8,128)(2,1)}), bf16[16,4,48,512]{3,2,1,0:T(8,128)(2,1)}, u32[]{:S(2)}, u32[]{:S(2)}) async-start(bf16[16,4,48,512]{3,2,1,0:T(8,128)(2,1)} %bitcast.79), calls=%async_computation | async-start | bytes 6291456 | tf_op jit(solution)/shard_map/all_to_all | solution.py:42
  30.8 0.0 copy-done.12
  30.8 0.9 convert_element_type.62
  31.7 0.0 copy-done.13
  31.7 0.1 copy.78
  31.8 12.2 %scatter_custom_fusion.1 = bf16[3072,512]{1,0:T(8,128)(2,1)} fusion(s32[2048]{0:T(1024)S(1)} %reshape.68, f32[256,512]{1,0:T(8,128)} %convert_element_type.62, f32[256,8]{1,0:T(8,128)S(1)} %copy.78, bf16[]{:T(256)} %constant.6.clone.1), kind=kCustom, calls=%fused_computation.24 | custom fusion | flops 2097152 | bytes 3801090 | tf_op jit(solution)/shard_map/scatter | solution.py:39
  44.0 29.3 %all-to-all-done = bf16[16,4,48,512]{3,2,1,0:T(8,128)(2,1)} async-done(((bf16[16,4,48,512]{3,2,1,0:T(8,128)(2,1)}), bf16[16,4,48,512]{3,2,1,0:T(8,128)(2,1)}, u32[]{:S(2)}, u32[]{:S(2)}) %all-to-all-start) | async-done | bytes 3145760 | tf_op jit(solution)/shard_map/all_to_all | solution.py:42
  73.3 7.9 %all-to-all-start.2 = ((bf16[16,4,48,512]{3,2,1,0:T(8,128)(2,1)}), bf16[16,4,48,512]{3,2,1,0:T(8,128)(2,1)}, u32[]{:S(2)}, u32[]{:S(2)}) async-start(bf16[16,4,48,512]{3,2,1,0:T(8,128)(2,1)} %bitcast.78), calls=%async_computation.2 | async-start | bytes 6291456 | tf_op jit(solution)/shard_map/all_to_all | solution.py:45
  81.2 0.5 all-reduce.3.cloned.1.call-start
  81.8 0.0 copy-start.15
  81.8 2.3 copy.72
  84.1 0.0 copy-start.8
  84.1 0.5 copy-done.15
  84.6 4.4 convolution_convert_fusion.1
  89.0 0.0 copy-done
  89.0 4.4 convolution_convert_fusion.2
  93.3 28.8 %all-to-all-done.2 = bf16[16,4,48,512]{3,2,1,0:T(8,128)(2,1)} async-done(((bf16[16,4,48,512]{3,2,1,0:T(8,128)(2,1)}), bf16[16,4,48,512]{3,2,1,0:T(8,128)(2,1)}, u32[]{:S(2)}, u32[]{:S(2)}) %all-to-all-start.2) | async-done | bytes 3145760 | tf_op jit(solution)/shard_map/all_to_all | solution.py:45
  122.2 2.3 copy.79
  124.5 1.0 copy-done.7
  125.5 7.8 %pad_maximum_fusion = bf16[4,768,1536]{1,2,0:T(8,128)(2,1)} fusion(bf16[4,768,768]{1,2,0:T(8,128)(2,1)S(1)} %copy-done.7, bf16[4,768,768]{1,2,0:T(8,128)(2,1)} %convolution_convert_fusion.2), kind=kLoop, calls=%fused_computation.10 | loop fusion | flops 18874368 | bytes 18874368 | tf_op jit(solution)/shard_map/concatenate | solution.py:51
  133.3 0.0 copy-done.10
  133.3 4.3 convolution_convert_fusion
  137.7 0.0 all-reduce.3.cloned.1.call-update
  137.7 158.2 %all-reduce.3.cloned.1.call-done = (bf16[4,768,1536]{1,2,0:T(8,128)(2,1)}, bf16[4,768,768]{1,2,0:T(8,128)(2,1)}) async-done(((bf16[4,768,1536]{1,2,0:T(8,128)(2,1)}, bf16[4,768,768]{1,2,0:T(8,128)(2,1)}), (bf16[4,768,1536]{1,2,0:T(8,128)(2,1)}, bf16[4,768,768]{1,2,0:T(8,128)(2,1)})) %all-reduce.3.cloned.1.call-update) | async-done | bytes 14155792 | tf_op jit(solution)/shard_map/psum | solution.py:58
  295.9 11.9 %convert_element_type.58 = f32[4,768,1536]{1,2,0:T(8,128)} convert(bf16[4,768,1536]{1,2,0:T(8,128)(2,1)} %get-tuple-element.6) | non-fusion elementwise | flops 4718592 | bytes 28311552 | tf_op jit(solution)/shard_map/convert_element_type | solution.py:58
  307.7 12.8 %fusion.3 = (bf16[4,768,768]{1,2,0:T(8,128)(2,1)S(1)}, bf16[4,768,768]{1,2,0:T(8,128)(2,1)S(1)}, bf16[4,768,768]{1,2,0:T(8,128)(2,1)}) fusion(bf16[4,768,768]{1,2,0:T(8,128)(2,1)} %get-tuple-element.7, f32[4,768,1536]{1,2,0:T(8,128)} %convert_element_type.58), kind=kLoop, calls=%fused_computation.9 | loop fusion | flops 37748736 | bytes 37748736 | tf_op jit(solution)/shard_map/convert_element_type | solution.py:19
  320.5 5.6 %fusion.21 = f32[4,768,512]{2,1,0:T(8,128)} fusion(bf16[4,768,768]{1,2,0:T(8,128)(2,1)S(1)} %get-tuple-element.9, bf16[4,512,768]{2,1,0:T(8,128)(2,1)S(1)} %copy-done), kind=kOutput, calls=%fused_computation.50 | convolution fusion | flops 2415919104 | bytes 14155776 | tf_op jit(solution)/shard_map/erf,edf->erd/dot_general | solution.py:87
  326.1 0.4 copy-done.6
  326.5 5.6 %add_convert_fusion = bf16[4,768,512]{2,1,0:T(8,128)(2,1)S(1)} fusion(f32[4,768,512]{2,1,0:T(8,128)} %fusion.21, bf16[4,768,768]{1,2,0:T(8,128)(2,1)S(1)} %get-tuple-element.8, bf16[4,512,768]{2,1,0:T(8,128)(2,1)S(1)} %copy-done.16), kind=kOutput, calls=%fused_computation.14 | convolution fusion | flops 2419064832 | bytes 17301504 | tf_op jit(solution)/shard_map/erf,edf->erd/dot_general | solution.py:88
  332.1 4.1 copy.83
  336.2 6.9 %all-to-all-start.3 = ((bf16[4,768,512]{2,0,1:T(4,128)(2,1)}), bf16[4,768,512]{2,0,1:T(4,128)(2,1)S(1)}, u32[]{:S(2)}, u32[]{:S(2)}) async-start(bf16[4,768,512]{2,0,1:T(4,128)(2,1)} %copy.83), calls=%async_computation.3 | async-start | bytes 6291456 | tf_op jit(solution)/shard_map/all_to_all | solution.py:90
  343.2 6.0 %convolution_convert_fusion.6 = bf16[4,768,512]{2,1,0:T(8,128)(2,1)S(1)} fusion(bf16[4,768,768]{1,2,0:T(8,128)(2,1)} %get-tuple-element.10, bf16[4,768,512]{2,1,0:T(8,128)(2,1)} %param.12), kind=kOutput, calls=%fused_computation.22 | convolution fusion | flops 2417491968 | bytes 11010048 | tf_op jit(solution)/shard_map/erf,efd->erd/dot_general | solution.py:60
  349.2 4.1 copy.76
  353.3 32.9 %all-to-all-done.3 = bf16[4,768,512]{2,0,1:T(4,128)(2,1)S(1)} async-done(((bf16[4,768,512]{2,0,1:T(4,128)(2,1)}), bf16[4,768,512]{2,0,1:T(4,128)(2,1)S(1)}, u32[]{:S(2)}, u32[]{:S(2)}) %all-to-all-start.3) | async-done | bytes 3145760 | tf_op jit(solution)/shard_map/all_to_all | solution.py:90
  386.2 1.7 copy-done.2
  387.9 5.3 %all-to-all-start.1 = ((bf16[4,768,512]{2,0,1:T(4,128)(2,1)}), bf16[4,768,512]{2,0,1:T(4,128)(2,1)}, u32[]{:S(2)}, u32[]{:S(2)}) async-start(bf16[4,768,512]{2,0,1:T(4,128)(2,1)} %copy.76), calls=%async_computation.1 | async-start | bytes 6291456 | tf_op jit(solution)/shard_map/all_to_all | solution.py:63
  393.1 0.2 copy.92
  393.3 0.7 broadcast_clamp_fusion
  394.0 8.0 %convolution_convert_fusion.4 = bf16[4,512,768]{2,1,0:T(8,128)(2,1)} fusion(bf16[4,768,512]{2,1,0:T(8,128)(2,1)} %bitcast.84, bf16[4,768,768]{1,2,0:T(8,128)(2,1)} %copy-done.6), kind=kOutput, calls=%fused_computation.20 | convolution fusion | flops 2417491968 | bytes 11010048 | tf_op jit(solution)/shard_map/erd,erf->edf/dot_general | solution.py:83
  402.0 6.7 %convolution_convert_fusion.5 = bf16[4,512,768]{2,1,0:T(8,128)(2,1)} fusion(bf16[4,768,512]{2,1,0:T(8,128)(2,1)S(1)} %bitcast.85, bf16[4,768,768]{1,2,0:T(8,128)(2,1)} %copy-done.5), kind=kOutput, calls=%fused_computation.21 | convolution fusion | flops 2417491968 | bytes 11010048 | tf_op jit(solution)/shard_map/erd,erf->edf/dot_general | solution.py:80
  408.7 3.9 convolution_convert_fusion.3
  412.7 0.9 copy.84
  413.6 9.2 %gather_fusion.1 = bf16[2048,512]{1,0:T(8,128)(2,1)} fusion(bf16[3072,512]{1,0:T(8,128)(2,1)S(1)} %bitcast.76, s32[2048]{0:T(1024)S(1)} %broadcast_clamp_fusion), kind=kCustom, calls=%fused_computation.1 | custom fusion | bytes 4202496 | tf_op jit(solution)/shard_map/gather | solution.py:93
  422.8 3.7 bitcast_reduce_fusion
  426.5 5.8 %all-to-all-done.1 = bf16[4,768,512]{2,0,1:T(4,128)(2,1)} async-done(((bf16[4,768,512]{2,0,1:T(4,128)(2,1)}), bf16[4,768,512]{2,0,1:T(4,128)(2,1)}, u32[]{:S(2)}, u32[]{:S(2)}) %all-to-all-start.1) | async-done | bytes 3145760 | tf_op jit(solution)/shard_map/all_to_all | solution.py:63
  432.3 2.8 copy.77
  435.1 9.2 %gather_fusion = bf16[2048,512]{1,0:T(8,128)(2,1)} fusion(bf16[3072,512]{1,0:T(8,128)(2,1)S(1)} %bitcast.75, s32[2048]{0:T(1024)S(1)} %broadcast_clamp_fusion), kind=kCustom, calls=%fused_computation | custom fusion | bytes 4202496 | tf_op jit(solution)/shard_map/gather | solution.py:66
  444.3 2.4 fusion.8
  446.7 0.7 copy.110
  447.5 1.0 fusion.10
  448.5 0.1 copy.98
  448.5 17.8 %psum.23 = bf16[256,8]{0,1:T(8,128)(2,1)S(1)} all-reduce(bf16[256,8]{0,1:T(8,128)(2,1)S(1)} %bitcast.91), channel_id=1, replica_groups=mesh['dp'=8,'expert'=16] {'dp'}, use_global_device_ids=true, to_apply=%region_9.10 | all-reduce | flops 2048 | bytes 8192 | tf_op jit(solution)/shard_map/psum | solution.py:75
  466.4 0.6 convert_element_type.70
  (32 shorter events, 0.1 us)
Async XLA Ops:
  7.2 81.8 %copy-start = (bf16[4,512,768]{2,1,0:T(8,128)(2,1)S(1)}, bf16[4,512,768]{2,1,0:T(8,128)(2,1)}, u32[]{:S(2)}) copy-start(bf16[4,512,768]{2,1,0:T(8,128)(2,1)} %param.10) | copy-start | bytes 9437188
  10.8 21.0 %copy-start.14 = (s32[2048]{0:T(1024)}, s32[2048]{0:T(1024)S(1)}, u32[]{:S(2)}) copy-start(s32[2048]{0:T(1024)S(1)} %reshape.68) | copy-start | bytes 24580
  22.7 8.2 %copy-start.12 = (bf16[256,512]{1,0:T(8,128)(2,1)S(1)}, bf16[256,512]{1,0:T(8,128)(2,1)}, u32[]{:S(2)}) copy-start(bf16[256,512]{1,0:T(8,128)(2,1)} %param.13) | copy-start | bytes 786436
  22.7 9.0 %copy-start.13 = (f32[256,8]{0,1:T(8,128)S(1)}, f32[256,8]{0,1:T(8,128)}, u32[]{:S(2)}) copy-start(f32[256,8]{0,1:T(8,128)} %param.9) | copy-start | bytes 24580
  22.7 50.7 %all-to-all-start = ((bf16[16,4,48,512]{3,2,1,0:T(8,128)(2,1)}), bf16[16,4,48,512]{3,2,1,0:T(8,128)(2,1)}, u32[]{:S(2)}, u32[]{:S(2)}) async-start(bf16[16,4,48,512]{3,2,1,0:T(8,128)(2,1)} %bitcast.79), calls=%async_computation | async-start | bytes 6291456 | tf_op jit(solution)/shard_map/all_to_all | solution.py:42
  73.3 48.9 %all-to-all-start.2 = ((bf16[16,4,48,512]{3,2,1,0:T(8,128)(2,1)}), bf16[16,4,48,512]{3,2,1,0:T(8,128)(2,1)}, u32[]{:S(2)}, u32[]{:S(2)}) async-start(bf16[16,4,48,512]{3,2,1,0:T(8,128)(2,1)} %bitcast.78), calls=%async_computation.2 | async-start | bytes 6291456 | tf_op jit(solution)/shard_map/all_to_all | solution.py:45
  81.2 214.6 %all-reduce.3.cloned.1.call-start = ((), (), s32[]{:S(2)}) async-start(), calls=%async_computation.4 | async-start | bytes 28311552 | tf_op jit(solution)/shard_map/psum | solution.py:58
  81.8 2.8 copy-start.15
  84.1 4.9 %copy-start.8 = (bf16[1,4,16,48,512]{4,3,2,1,0:T(8,128)(2,1)}, bf16[1,4,16,48,512]{4,3,2,1,0:T(8,128)(2,1)S(1)}, u32[]{:S(2)}) copy-start(bf16[1,4,16,48,512]{4,3,2,1,0:T(8,128)(2,1)S(1)} %copy.72) | copy-start | bytes 9437188
  122.2 3.3 copy-start.7
  125.5 7.8 %copy-start.10 = (bf16[1,4,16,48,512]{4,3,2,1,0:T(8,128)(2,1)}, bf16[1,4,16,48,512]{4,3,2,1,0:T(8,128)(2,1)S(1)}, u32[]{:S(2)}) copy-start(bf16[1,4,16,48,512]{4,3,2,1,0:T(8,128)(2,1)S(1)} %copy.79) | copy-start | bytes 9437188
  125.5 7.8 %copy-start.17 = (bf16[4,768,512]{2,1,0:T(8,128)(2,1)S(1)}, bf16[4,768,512]{2,1,0:T(8,128)(2,1)}, u32[]{:S(2)}) copy-start(bf16[4,768,512]{2,1,0:T(8,128)(2,1)} %param.12) | copy-start | bytes 9437188
  320.5 5.6 %copy-start.5 = (bf16[4,768,768]{1,2,0:T(8,128)(2,1)}, bf16[4,768,768]{1,2,0:T(8,128)(2,1)S(1)}, u32[]{:S(2)}) copy-start(bf16[4,768,768]{1,2,0:T(8,128)(2,1)S(1)} %get-tuple-element.9) | copy-start | bytes 14155780
  320.5 6.0 %copy-start.6 = (bf16[4,768,768]{1,2,0:T(8,128)(2,1)}, bf16[4,768,768]{1,2,0:T(8,128)(2,1)S(1)}, u32[]{:S(2)}) copy-start(bf16[4,768,768]{1,2,0:T(8,128)(2,1)S(1)} %get-tuple-element.8) | copy-start | bytes 14155780
  320.5 6.0 %copy-start.16 = (bf16[4,512,768]{2,1,0:T(8,128)(2,1)S(1)}, bf16[4,512,768]{2,1,0:T(8,128)(2,1)}, u32[]{:S(2)}) copy-start(bf16[4,512,768]{2,1,0:T(8,128)(2,1)} %param.11) | copy-start | bytes 9437188
  336.2 49.9 %all-to-all-start.3 = ((bf16[4,768,512]{2,0,1:T(4,128)(2,1)}), bf16[4,768,512]{2,0,1:T(4,128)(2,1)S(1)}, u32[]{:S(2)}, u32[]{:S(2)}) async-start(bf16[4,768,512]{2,0,1:T(4,128)(2,1)} %copy.83), calls=%async_computation.3 | async-start | bytes 6291456 | tf_op jit(solution)/shard_map/all_to_all | solution.py:90
  386.2 1.7 copy-start.2
  387.9 44.4 %all-to-all-start.1 = ((bf16[4,768,512]{2,0,1:T(4,128)(2,1)}), bf16[4,768,512]{2,0,1:T(4,128)(2,1)}, u32[]{:S(2)}, u32[]{:S(2)}) async-start(bf16[4,768,512]{2,0,1:T(4,128)(2,1)} %copy.76), calls=%async_computation.1 | async-start | bytes 6291456 | tf_op jit(solution)/shard_map/all_to_all | solution.py:63
  394.0 8.0 %copy-start.9 = (bf16[1,4,16,48,512]{4,3,2,1,0:T(8,128)(2,1)S(1)}, bf16[1,4,16,48,512]{4,3,2,1,0:T(8,128)(2,1)}, u32[]{:S(2)}) copy-start(bf16[1,4,16,48,512]{4,3,2,1,0:T(8,128)(2,1)} %copy-done.8) | copy-start | bytes 9437188
  394.0 14.7 %slice-start = ((s8[4718592]{0:T(1024)(128)(4,1)}), s8[4194304]{0:T(1024)(128)(4,1)S(1)}, s32[]{:S(2)}) async-start(s8[4718592]{0:T(1024)(128)(4,1)} %bitcast.80), calls=%async_computation.5 | async-start | bytes 8388608
  402.0 6.7 %slice-start.1 = ((s8[4718592]{0:T(1024)(128)(4,1)}), s8[524288]{0:T(1024)(128)(4,1)S(1)}, s32[]{:S(2)}) async-start(s8[4718592]{0:T(1024)(128)(4,1)} %bitcast.80), calls=%async_computation.6 | async-start | bytes 1048576
  402.0 6.7 %copy-start.11 = (bf16[1,4,16,48,512]{4,3,2,1,0:T(8,128)(2,1)S(1)}, bf16[1,4,16,48,512]{4,3,2,1,0:T(8,128)(2,1)}, u32[]{:S(2)}) copy-start(bf16[1,4,16,48,512]{4,3,2,1,0:T(8,128)(2,1)} %copy-done.10) | copy-start | bytes 9437188
  408.7 4.0 copy-start.3
  444.3 3.2 copy-start.4
  444.3 22.7 %copy-start.1 = (bf16[4,512,768]{2,1,0:T(8,128)(2,1)S(1)}, bf16[4,512,768]{2,1,0:T(8,128)(2,1)}, u32[]{:S(2)}) copy-start(bf16[4,512,768]{2,1,0:T(8,128)(2,1)} %param.10) | copy-start | bytes 9437188
Sparse Core Ops, SparseCore 0:
  137.8 158.0 all-reduce.2
where the time goes:
time: 483 us; the launch traced here: 474 us
  waiting for transfers between devices  255 us (53%)
  other arithmetic  53.7 us (11%)
  matrix products  52.3 us (11%)
  local copies, waits for them, and re-layouts  51.9 us (11%)
  starting transfers between devices  28.8 us (6%)
  blocking collectives  17.8 us (4%)
  between operations  14.5 us (3%)
    psum x1, waiting for transfers between devices, local(): lax.psum(partial_value.astype(jnp.bfloat16), 'dp').astype(jnp.float32)  158 us
    all_to_all x1, waiting for transfers between devices, local(): lax.all_to_all(slot_grad_out, 'expert', split_axis=1, concat_axis=0, tile...  32.9 us
    all_to_all x1, waiting for transfers between devices, local(): lax.all_to_all(sent_rows.reshape(layout), 'expert', split_axis=0, concat_...  29.3 us
    all_to_all x1, waiting for transfers between devices, local(): lax.all_to_all(sent_grads.reshape(layout), 'expert', split_axis=0, concat...  28.8 us
    psum x1, blocking collectives, local(): lax.psum(router_part.astype(jnp.bfloat16), 'dp').astype(jnp.float32)  17.8 us
    convert_element_type x1, other arithmetic, derive(): d_up.astype(jnp.bfloat16)  12.8 us
    scatter x1, other arithmetic, local(): jnp.zeros((experts * capacity, width_part), jnp.bfloat16).at[slot]  12.2 us
    scatter x1, local copies, waits for them, and re-layouts, local(): jnp.zeros((experts * capacity, width_part), jnp.bfloat16).at[slot]  11.9 us
  transfers between devices with their start and end apart: 5, of which 5 were waited for; matrix products, arithmetic and copies ran while one was open for 14% of the time, Pallas kernels for 0%

commit v1 on v0

v1 whole, which is shorter than its diff:
```python
import jax
import jax.numpy as jnp
from jax import lax
from jax.sharding import PartitionSpec as P

F32 = jnp.float32
BF16 = jnp.bfloat16


def local(tokens, expert_ids, route_weights, w_gate, w_up, w_down, out_grad):
    tok, top = expert_ids.shape
    e_loc, width, ff = w_gate.shape
    owners = lax.axis_size("expert")
    n_dp = lax.axis_size("dp")
    experts = e_loc * owners
    cap = 3 * tok * top // (2 * experts)
    rows = owners * cap
    table = jnp.arange(experts, dtype=jnp.int32)
    hit = expert_ids[:, None, :] == table[None, :, None]
    member = jnp.any(hit, 2)
    tri = (jnp.arange(tok)[:, None] > jnp.arange(tok)[None, :]).astype(BF16)
    before = jnp.dot(tri, member.astype(BF16), preferred_element_type=F32).astype(jnp.int32)
    rank = jnp.where(member, before, -1)
    weight = jnp.sum(jnp.where(hit, route_weights[:, None, :], 0.0), 2).astype(BF16)
    pick = rank.T[:, None, :] == jnp.arange(cap, dtype=jnp.int32)[None, :, None]
    one = pick.astype(BF16).reshape(experts * cap, tok)
    scaled = jnp.where(pick, weight.T[:, None, :], 0).astype(BF16).reshape(experts * cap, tok)
    layout = (owners, e_loc, cap, width)

    def out(v):
        return lax.all_to_all(v.reshape(layout), "expert", split_axis=0, concat_axis=2, tiled=True)[0]

    x = out(jnp.dot(one, tokens, preferred_element_type=F32).astype(BF16))
    g = out(jnp.dot(scaled, out_grad, preferred_element_type=F32).astype(BF16))
    part = jnp.concatenate(
        (
            jnp.einsum("erd,edf->erf", x, w_gate, preferred_element_type=F32).astype(BF16),
            jnp.einsum("erd,edf->erf", x, w_up, preferred_element_type=F32).astype(BF16),
            jnp.einsum("erd,efd->erf", g, w_down, preferred_element_type=F32).astype(BF16),
        ),
        -1,
    )
    full = lax.psum_scatter(part, "dp", scatter_dimension=1, tiled=True).astype(F32)
    gate, up, gh = full[..., :ff], full[..., ff : 2 * ff], full[..., 2 * ff :]
    sig = jax.nn.sigmoid(gate)
    act = gate * sig
    hid = (act * up).astype(BF16)
    dg = (gh * up * sig * (1.0 + gate * (1.0 - sig))).astype(BF16)
    du = (gh * act).astype(BF16)
    route = jnp.sum(hid.astype(F32) * gh, -1)
    every = lax.all_gather(jnp.concatenate((hid, dg, du), -1), "dp", axis=1, tiled=True)
    hid, dg, du = every[..., :ff], every[..., ff : 2 * ff], every[..., 2 * ff :]
    eo = jnp.einsum("erf,efd->erd", hid, w_down, preferred_element_type=F32).astype(BF16)
    so = (
        jnp.einsum("erf,edf->erd", dg, w_gate, preferred_element_type=F32)
        + jnp.einsum("erf,edf->erd", du, w_up, preferred_element_type=F32)
    ).astype(BF16)

    def back(v):
        v = lax.all_to_all(v, "expert", split_axis=1, concat_axis=0, tiled=True)
        return v.reshape(experts * cap, -1)

    mixed = jnp.einsum("st,sd->td", scaled, back(eo), preferred_element_type=F32).astype(BF16)
    grad_tokens = jnp.einsum("st,sd->td", one, back(so), preferred_element_type=F32).astype(BF16)
    grad_down = jnp.einsum("erf,erd->efd", hid, g, preferred_element_type=F32).astype(BF16)
    grad_gate = jnp.einsum("erd,erf->edf", x, dg, preferred_element_type=F32).astype(BF16)
    grad_up = jnp.einsum("erd,erf->edf", x, du, preferred_element_type=F32).astype(BF16)
    route = lax.all_gather(lax.all_gather(route, "dp", axis=1, tiled=True), "expert", axis=0, tiled=True)
    mine = lax.dynamic_slice_in_dim(route, lax.axis_index("expert") * cap, cap, 1)
    per = jnp.sum(jnp.where(pick, mine[:, :, None], 0.0), 1)
    grad_route = jnp.sum(jnp.where(hit, per.T[:, :, None], 0.0), 1)
    grad_route = grad_route / route_weights.astype(BF16).astype(F32)
    return (mixed, grad_tokens, grad_route, grad_gate, grad_up, grad_down)


def solution(mesh):
    tok = P("expert", "dp")
    whole = P("expert", None)
    wide = P("expert", "dp", None)
    down = P("expert", None, "dp")
    return jax.shard_map(
        local,
        mesh=mesh,
        in_specs=(tok, whole, whole, wide, wide, down, tok),
        out_specs=(tok, tok, whole, wide, wide, down),
        check_vma=False,
    )
```

time: 483 us -> 582 us (1.20)
  waiting for transfers between devices: 255 us -> 330 us
  blocking collectives: 17.8 us -> 54.2 us
  other arithmetic: 53.7 us -> 22.8 us
  local copies, waits for them, and re-layouts: 51.9 us -> 61.9 us
    psum x1 -> x0, waiting for transfers between devices: 158 us -> none  [local(): lax.psum(partial_value.astype(jnp.bfloat16), 'dp').astype(jnp.float32)]
    unnamed x1 -> x3, waiting for transfers between devices: 0.02 us -> 156 us
    all_gather x0 -> x1, waiting for transfers between devices: none -> 74 us  [local(): lax.all_gather(jnp.concatenate((hid, dg, du), -1), 'dp', axis=1, tiled=True)]
    all_gather x0 -> x2, blocking collectives: none -> 54.2 us  [the longest x1 43 us: local(): lax.all_gather(lax.all_gather(route, 'dp', axis=1, tiled=True), 'expert',...]
    convert_element_type x4 -> x1, other arithmetic: 26.1 us -> 0.28 us  [local(): lax.psum_scatter(part, 'dp', scatter_dimension=1, tiled=True).astype(F32)]
    concatenate x0 -> x2, local copies, waits for them, and re-layouts: none -> 25.2 us  [the longest x1 22.6 us: local(): jnp.concatenate((jnp.einsum('erd,edf->erf', x, w_gate, preferred_element_...]
    gather x2 -> x0, local copies, waits for them, and re-layouts: 18.4 us -> none  [the longest x1 9.22 us: local(): picked = returned[slot].astype(jnp.float32)]
    psum x1 -> x0, blocking collectives: 17.8 us -> none  [local(): lax.psum(router_part.astype(jnp.bfloat16), 'dp').astype(jnp.float32)]
  transfers between devices with their start and end apart: 5 -> 6, of which waited for: 5 -> 5; matrix products, arithmetic and copies ran while one was open for 14% -> 9% of each run, Pallas kernels for 0% -> 0%
where the time goes in v1:
time: 582 us; the launch traced here: 573 us
  waiting for transfers between devices  330 us (57%)
  local copies, waits for them, and re-layouts  61.9 us (11%)
  matrix products  55 us (9%)
  blocking collectives  54.2 us (9%)
  starting transfers between devices  34.2 us (6%)
  other arithmetic  22.8 us (4%)
  between operations  15.3 us (3%)
    unnamed x3, waiting for transfers between devices  156 us
    all_gather x1, waiting for transfers between devices, local(): lax.all_gather(jnp.concatenate((hid, dg, du), -1), 'dp', axis=1, tiled=True)  74 us
    all_to_all x2, waiting for transfers between devices, out(): lax.all_to_all(v.reshape(layout), 'expert', split_axis=0, concat_axis=2,...  69.1 us
    all_gather x1, blocking collectives, local(): lax.all_gather(lax.all_gather(route, 'dp', axis=1, tiled=True), 'expert',...  43 us
    all_to_all x2, waiting for transfers between devices, back(): v = lax.all_to_all(v, 'expert', split_axis=1, concat_axis=0, tiled=True)  30.5 us
    concatenate x1, local copies, waits for them, and re-layouts, local(): jnp.concatenate((jnp.einsum('erd,edf->erf', x, w_gate, preferred_element_...  22.6 us
    all_to_all x2, starting transfers between devices, back(): v = lax.all_to_all(v, 'expert', split_axis=1, concat_axis=0, tiled=True)  17.6 us
    all_to_all x2, starting transfers between devices, out(): lax.all_to_all(v.reshape(layout), 'expert', split_axis=0, concat_axis=2,...  16 us
  transfers between devices with their start and end apart: 6, of which 5 were waited for; matrix products, arithmetic and copies ran while one was open for 9% of the time, Pallas kernels for 0%

profile of v1, /device:TPU:0, one launch (start us, length us, event | category | flops | bytes accessed | tf_op | source)
XLA Modules:
  0.0 573.2 jit_solution(3746814541814262817)
XLA Ops:
  7.2 1.0 fusion.29
  8.2 0.2 fusion.28
  8.4 0.1 eq.62
  8.5 0.5 bitcast_compare_fusion
  9.0 3.6 convolution_convert_fusion.1
  12.6 8.1 %all-to-all-start = ((bf16[16,4,48,512]{3,2,1,0:T(8,128)(2,1)}), bf16[16,4,48,512]{3,2,1,0:T(8,128)(2,1)}, u32[]{:S(2)}, u32[]{:S(2)}) async-start(bf16[16,4,48,512]{3,2,1,0:T(8,128)(2,1)} %bitcast.62), calls=%async_computation | async-start | bytes 6291456 | tf_op jit(solution)/shard_map/all_to_all | solution.py:31
  20.8 0.2 select_reduce_fusion.2
  20.9 0.5 bitcast_select_fusion
  21.4 2.6 convolution_convert_fusion
  24.1 39.2 %all-to-all-done = bf16[16,4,48,512]{3,2,1,0:T(8,128)(2,1)} async-done(((bf16[16,4,48,512]{3,2,1,0:T(8,128)(2,1)}), bf16[16,4,48,512]{3,2,1,0:T(8,128)(2,1)}, u32[]{:S(2)}, u32[]{:S(2)}) %all-to-all-start) | async-done | bytes 3145760 | tf_op jit(solution)/shard_map/all_to_all | solution.py:31
  63.3 7.9 %all-to-all-start.1 = ((bf16[16,4,48,512]{3,2,1,0:T(8,128)(2,1)}), bf16[16,4,48,512]{3,2,1,0:T(8,128)(2,1)}, u32[]{:S(2)}, u32[]{:S(2)}) async-start(bf16[16,4,48,512]{3,2,1,0:T(8,128)(2,1)} %bitcast.63), calls=%async_computation.1 | async-start | bytes 6291456 | tf_op jit(solution)/shard_map/all_to_all | solution.py:31
  71.2 0.0 all-reduce.3.cloned.1.call-start
  71.2 2.2 copy.116
  73.4 4.3 convolution_convert_fusion.3
  77.8 4.4 convolution_convert_fusion.4
  82.2 29.9 %all-to-all-done.1 = bf16[16,4,48,512]{3,2,1,0:T(8,128)(2,1)} async-done(((bf16[16,4,48,512]{3,2,1,0:T(8,128)(2,1)}), bf16[16,4,48,512]{3,2,1,0:T(8,128)(2,1)}, u32[]{:S(2)}, u32[]{:S(2)}) %all-to-all-start.1) | async-done | bytes 3145760 | tf_op jit(solution)/shard_map/all_to_all | solution.py:31
  112.1 2.3 copy.119
  114.5 6.4 %convolution_convert_fusion.2 = bf16[4,768,768]{1,2,0:T(8,128)(2,1)S(1)} fusion(bf16[4,768,512]{2,1,0:T(8,128)(2,1)S(1)} %bitcast.76, bf16[4,768,512]{2,1,0:T(8,128)(2,1)} %param.12), kind=kOutput, calls=%fused_computation.19 | convolution fusion | flops 2418278400 | bytes 11010048 | tf_op jit(solution)/shard_map/erd,efd->erf/dot_general | solution.py:39
  121.0 14.7 %pad_maximum_fusion = bf16[4,768,2304]{1,2,0:T(8,128)(2,1)} fusion(bf16[4,768,768]{1,2,0:T(8,128)(2,1)S(1)} %convolution_convert_fusion.2, bf16[4,768,768]{1,2,0:T(8,128)(2,1)S(1)} %bitcast.69, bf16[4,768,768]{1,2,0:T(8,128)(2,1)S(1)} %bitcast.71), kind=kLoop, calls=%fused_computation | loop fusion | flops 42467328 | bytes 28311552 | tf_op jit(solution)/shard_map/concatenate | solution.py:35
  135.7 22.6 %copy.120 = bf16[4,768,2304]{2,0,1:T(4,128)(2,1)} copy(bf16[4,768,2304]{1,2,0:T(8,128)(2,1)} %pad_maximum_fusion) | data formatting | bytes 28311552 | tf_op jit(solution)/shard_map/concatenate | solution.py:35
  158.3 0.5 all-gather.4.cloned.1.call-start
  158.8 0.1 copy-done.16
  158.9 0.6 dynamic-slice
  160.2 156.1 %all-reduce.3.cloned.1.call-done = bf16[4,768,2304]{2,0,1:T(4,128)(2,1)} async-done(((bf16[4,768,2304]{2,0,1:T(4,128)(2,1)}), bf16[4,768,2304]{2,0,1:T(4,128)(2,1)}) %all-reduce.3.cloned.1.call-update) | async-done | bytes 14155792
  316.3 2.1 constant_dynamic-slice_fusion
  318.4 0.3 copy_convert_fusion
  318.7 0.8 multiply_reduce_fusion
  319.5 0.1 pad_maximum_fusion.1
  319.6 2.6 copy.122
  322.2 74.0 %all-gather.4.cloned.1.call-done = bf16[4,768,2304]{2,0,1:T(4,128)(2,1)} async-done(((bf16[4,96,2304]{2,0,1:T(4,128)(2,1)}), bf16[4,768,2304]{2,0,1:T(4,128)(2,1)}) %all-gather.4.cloned.1.call-update) | async-done | bytes 14155792 | tf_op jit(solution)/shard_map/all_gather | solution.py:51
  396.2 10.6 %fusion.30 = (bf16[4,768,768]{2,0,1:T(4,128)(2,1)S(1)}, bf16[4,768,768]{2,0,1:T(4,128)(2,1)}, bf16[4,768,768]{2,0,1:T(4,128)(2,1)S(1)}) fusion(bf16[4,768,2304]{2,0,1:T(4,128)(2,1)} %all-gather.4.cloned.1.call-done), kind=kLoop, calls=%fused_computation.49 | loop fusion | bytes 28311552 | tf_op jit(solution)/shard_map/slice | solution.py:52
  406.7 2.6 fusion.2
  409.4 1.5 copy-done.3
  410.9 0.0 copy-done.15
  410.9 2.9 add_convert_fusion
  413.8 4.1 copy.129
  417.9 7.1 %all-to-all-start.3 = ((bf16[4,768,512]{2,0,1:T(4,128)(2,1)}), bf16[4,768,512]{2,0,1:T(4,128)(2,1)S(1)}, u32[]{:S(2)}, u32[]{:S(2)}) async-start(bf16[4,768,512]{2,0,1:T(4,128)(2,1)} %copy.129), calls=%async_computation.3 | async-start | bytes 6291456 | tf_op jit(solution)/shard_map/all_to_all | solution.py:60
  425.0 2.0 fusion.26
  427.0 5.9 %fusion.12 = bf16[4,768,512]{2,1,0:T(8,128)(2,1)S(1)} fusion(bf16[4,768,512]{2,1,0:T(8,128)(2,1)} %param.12, bf16[4,768,768]{2,0,1:T(4,128)(2,1)} %get-tuple-element.9), kind=kOutput, calls=%fused_computation.22 | convolution fusion | flops 2417491968 | bytes 11010048 | tf_op jit(solution)/shard_map/erf,efd->erd/dot_general | solution.py:53
  432.9 4.1 copy.124
  437.1 30.5 %all-to-all-done.3 = bf16[4,768,512]{2,0,1:T(4,128)(2,1)S(1)} async-done(((bf16[4,768,512]{2,0,1:T(4,128)(2,1)}), bf16[4,768,512]{2,0,1:T(4,128)(2,1)S(1)}, u32[]{:S(2)}, u32[]{:S(2)}) %all-to-all-start.3) | async-done | bytes 3145760 | tf_op jit(solution)/shard_map/all_to_all | solution.py:60
  467.6 10.5 %all-to-all-start.2 = ((bf16[4,768,512]{2,0,1:T(4,128)(2,1)}), bf16[4,768,512]{2,0,1:T(4,128)(2,1)}, u32[]{:S(2)}, u32[]{:S(2)}) async-start(bf16[4,768,512]{2,0,1:T(4,128)(2,1)} %copy.124), calls=%async_computation.2 | async-start | bytes 6291456 | tf_op jit(solution)/shard_map/all_to_all | solution.py:60
  478.1 1.4 iota_compare_fusion
  479.5 0.1 copy.143
  479.6 0.1 copy.133
  479.6 11.2 %all-gather = f32[8,96,4]{1,2,0:T(4,128)S(1)} all-gather(f32[1,96,4]{1,2,0:T(4,128)S(1)} %copy.133), channel_id=1, replica_groups=mesh['dp'=8,'expert'=16] {'dp'}, dimensions={0}, use_global_device_ids=true | all-gather | bytes 13824 | tf_op jit(solution)/shard_map/all_gather | solution.py:68
  490.9 0.1 reshape.109
  491.0 43.0 %all-gather.1 = f32[16,4,768]{2,1,0:T(4,128)S(1)} all-gather(f32[1,4,768]{2,1,0:T(4,128)S(1)} %bitcast.86), channel_id=1, replica_groups=mesh['dp'=8,'expert'=16] {'expert'}, dimensions={0}, use_global_device_ids=true | all-gather | bytes 208896 | tf_op jit(solution)/shard_map/all_gather | solution.py:68
  534.0 0.7 reshape.111
  534.7 0.9 constant_dynamic-slice_fusion.1
  535.6 0.7 select_reduce_fusion
  536.3 0.1 select_reduce_fusion.1
  536.4 0.6 convert_divide_fusion
  537.0 7.8 %fusion.18 = bf16[4,512,768]{2,1,0:T(8,128)(2,1)} fusion(bf16[4,768,512]{2,1,0:T(8,128)(2,1)} %bitcast.74, bf16[4,768,768]{2,0,1:T(4,128)(2,1)} %copy-done.3), kind=kOutput, calls=%fused_computation.24 | convolution fusion | flops 2417491968 | bytes 11010048 | tf_op jit(solution)/shard_map/erd,erf->edf/dot_general | solution.py:66
  544.8 6.6 %fusion.21 = bf16[4,512,768]{2,1,0:T(8,128)(2,1)} fusion(bf16[4,768,512]{2,1,0:T(8,128)(2,1)S(1)} %bitcast.75, bf16[4,768,768]{2,0,1:T(4,128)(2,1)} %copy-done.2), kind=kOutput, calls=%fused_computation.25 | convolution fusion | flops 2417491968 | bytes 11010048 | tf_op jit(solution)/shard_map/erd,erf->edf/dot_general | solution.py:67
  551.4 4.0 fusion.15
  555.5 0.6 copy.130
  556.1 1.9 copy.131
  558.1 2.5 copy.125
  560.6 0.3 copy.126
  560.9 1.6 copy-done.8
  562.5 0.2 copy-done.10
  562.7 1.7 convolution_convert_fusion.5
  564.4 1.7 convolution_convert_fusion.6
  (49 shorter events, 0.1 us)
Async XLA Ops:
  7.2 66.2 %copy-start = (bf16[4,512,768]{2,1,0:T(8,128)(2,1)S(1)}, bf16[4,512,768]{2,1,0:T(8,128)(2,1)}, u32[]{:S(2)}) copy-start(bf16[4,512,768]{2,1,0:T(8,128)(2,1)} %param.11) | copy-start | bytes 9437188
  12.6 8.2 %copy-start.12 = (s32[256,8]{0,1:T(8,128)S(1)}, s32[256,8]{0,1:T(8,128)}, u32[]{:S(2)}) copy-start(s32[256,8]{0,1:T(8,128)} %param.8) | copy-start | bytes 24580
  12.6 8.2 %copy-start.13 = (f32[256,8]{0,1:T(8,128)S(1)}, f32[256,8]{0,1:T(8,128)}, u32[]{:S(2)}) copy-start(f32[256,8]{0,1:T(8,128)} %param.9) | copy-start | bytes 24580
  12.6 8.8 %copy-start.11 = (bf16[256,512]{1,0:T(8,128)(2,1)S(1)}, bf16[256,512]{1,0:T(8,128)(2,1)}, u32[]{:S(2)}) copy-start(bf16[256,512]{1,0:T(8,128)(2,1)} %param.13) | copy-start | bytes 786436
  12.6 50.7 %all-to-all-start = ((bf16[16,4,48,512]{3,2,1,0:T(8,128)(2,1)}), bf16[16,4,48,512]{3,2,1,0:T(8,128)(2,1)}, u32[]{:S(2)}, u32[]{:S(2)}) async-start(bf16[16,4,48,512]{3,2,1,0:T(8,128)(2,1)} %bitcast.62), calls=%async_computation | async-start | bytes 6291456 | tf_op jit(solution)/shard_map/all_to_all | solution.py:31
  63.3 48.9 %all-to-all-start.1 = ((bf16[16,4,48,512]{3,2,1,0:T(8,128)(2,1)}), bf16[16,4,48,512]{3,2,1,0:T(8,128)(2,1)}, u32[]{:S(2)}, u32[]{:S(2)}) async-start(bf16[16,4,48,512]{3,2,1,0:T(8,128)(2,1)} %bitcast.63), calls=%async_computation.1 | async-start | bytes 6291456 | tf_op jit(solution)/shard_map/all_to_all | solution.py:31
  71.2 245.1 %all-reduce.3.cloned.1.call-start = ((), (), s32[]{:S(2)}) async-start(), calls=%async_computation.5 | async-start | bytes 28311552
  73.4 4.4 copy-start.4
  73.4 4.4 copy-start.14
  112.1 8.8 %slice-start.2 = ((s8[4718592]{0:T(1024)(128)(4,1)}), s8[4194304]{0:T(1024)(128)(4,1)S(1)}, s32[]{:S(2)}) async-start(s8[4718592]{0:T(1024)(128)(4,1)} %bitcast.68), calls=%async_computation.8 | async-start | bytes 8388608
  112.1 8.8 %slice-start.4 = ((s8[4718592]{0:T(1024)(128)(4,1)}), s8[4194304]{0:T(1024)(128)(4,1)S(1)}, s32[]{:S(2)}) async-start(s8[4718592]{0:T(1024)(128)(4,1)} %bitcast.70), calls=%async_computation.10 | async-start | bytes 8388608
  114.4 6.5 %copy-start.6 = (bf16[1,4,16,48,512]{4,3,2,1,0:T(8,128)(2,1)}, bf16[1,4,16,48,512]{4,3,2,1,0:T(8,128)(2,1)S(1)}, u32[]{:S(2)}) copy-start(bf16[1,4,16,48,512]{4,3,2,1,0:T(8,128)(2,1)S(1)} %copy.119) | copy-start | bytes 9437188
  114.4 6.5 %slice-start.3 = ((s8[4718592]{0:T(1024)(128)(4,1)}), s8[524288]{0:T(1024)(128)(4,1)S(1)}, s32[]{:S(2)}) async-start(s8[4718592]{0:T(1024)(128)(4,1)} %bitcast.68), calls=%async_computation.9 | async-start | bytes 1048576
  114.5 6.5 %slice-start.5 = ((s8[4718592]{0:T(1024)(128)(4,1)}), s8[524288]{0:T(1024)(128)(4,1)S(1)}, s32[]{:S(2)}) async-start(s8[4718592]{0:T(1024)(128)(4,1)} %bitcast.70), calls=%async_computation.11 | async-start | bytes 1048576
  158.3 0.7 copy-start.16
  158.3 237.9 %all-gather.4.cloned.1.call-start = ((), (), s32[]{:S(2)}) async-start(), calls=%async_computation.4 | async-start | bytes 15925248 | tf_op jit(solution)/shard_map/all_gather | solution.py:51
  406.7 2.7 copy-start.2
  406.7 4.1 copy-start.3
  406.7 4.2 copy-start.15
  417.9 49.7 %all-to-all-start.3 = ((bf16[4,768,512]{2,0,1:T(4,128)(2,1)}), bf16[4,768,512]{2,0,1:T(4,128)(2,1)S(1)}, u32[]{:S(2)}, u32[]{:S(2)}) async-start(bf16[4,768,512]{2,0,1:T(4,128)(2,1)} %copy.129), calls=%async_computation.3 | async-start | bytes 6291456 | tf_op jit(solution)/shard_map/all_to_all | solution.py:60
  467.6 90.5 %all-to-all-start.2 = ((bf16[4,768,512]{2,0,1:T(4,128)(2,1)}), bf16[4,768,512]{2,0,1:T(4,128)(2,1)}, u32[]{:S(2)}, u32[]{:S(2)}) async-start(bf16[4,768,512]{2,0,1:T(4,128)(2,1)} %copy.124), calls=%async_computation.2 | async-start | bytes 6291456 | tf_op jit(solution)/shard_map/all_to_all | solution.py:60
  537.0 7.8 %copy-start.5 = (bf16[1,4,16,48,512]{4,3,2,1,0:T(8,128)(2,1)S(1)}, bf16[1,4,16,48,512]{4,3,2,1,0:T(8,128)(2,1)}, u32[]{:S(2)}) copy-start(bf16[1,4,16,48,512]{4,3,2,1,0:T(8,128)(2,1)} %copy-done.4) | copy-start | bytes 9437188
  537.0 14.4 %slice-start = ((s8[4718592]{0:T(1024)(128)(4,1)}), s8[4194304]{0:T(1024)(128)(4,1)S(1)}, s32[]{:S(2)}) async-start(s8[4718592]{0:T(1024)(128)(4,1)} %bitcast.66), calls=%async_computation.6 | async-start | bytes 8388608
  544.8 6.6 %slice-start.1 = ((s8[4718592]{0:T(1024)(128)(4,1)}), s8[524288]{0:T(1024)(128)(4,1)S(1)}, s32[]{:S(2)}) async-start(s8[4718592]{0:T(1024)(128)(4,1)} %bitcast.66), calls=%async_computation.7 | async-start | bytes 1048576
  544.8 6.6 %copy-start.7 = (bf16[1,4,16,48,512]{4,3,2,1,0:T(8,128)(2,1)S(1)}, bf16[1,4,16,48,512]{4,3,2,1,0:T(8,128)(2,1)}, u32[]{:S(2)}) copy-start(bf16[1,4,16,48,512]{4,3,2,1,0:T(8,128)(2,1)} %copy-done.6) | copy-start | bytes 9437188
  560.6 1.9 copy-start.8
  560.6 2.1 copy-start.10
  562.7 1.7 copy-start.9
  562.7 3.4 copy-start.1
Sparse Core Ops, SparseCore 0:
  158.4 157.8 all-reduce.2
  322.3 73.8 all-gather.3

commit v2 on v1

v2 whole, which is shorter than its diff:
```python
import jax
import jax.numpy as jnp
from jax import lax
from jax.experimental import pallas as pl
from jax.experimental.pallas import tpu as pltpu
from jax.sharding import PartitionSpec as P

F32 = jnp.float32
BF16 = jnp.bfloat16
MESH = pl.DeviceIdType.MESH
NN = ((1,), (0,))
NT = ((1,), (1,))
TN = ((0,), (0,))


def dot(a, b, dims):
    return lax.dot_general(a, b, (dims, ((), ())), preferred_element_type=F32)


def kernel(
    rank_ref, weight_ref, tok_ref, og_ref, wg_hbm, wu_hbm, wd_hbm,
    mixed_ref, gtok_ref, route_ref, gg_hbm, gu_hbm, gd_hbm,
    wg, wu, wd, one, scaled, sent, xg, mine, held, far, act, back, st_g, st_u, st_d,
    acc_m, acc_t, dr_all, dr_in,
    w_sem, o_sem, d_send, d_recv, h_send, h_recv, r_send, r_recv, a_send, a_recv, c_send, c_recv,
    t_send, t_recv, q_send, q_recv, v_send, v_recv,
):
    n_e, _, rows, _ = sent.shape
    ff = wg.shape[2]
    n_o = lax.axis_size("expert")
    n_dp = lax.axis_size("dp")
    n_y = n_dp // 2
    cap = rows // n_o
    half = rows // 2
    part = half // n_y
    dp = lax.axis_index("dp")
    me = lax.axis_index("expert")
    y, core = dp // 2, dp % 2
    share = core * n_y + y
    own0 = pl.multiple_of(core * half, half)
    other0 = pl.multiple_of((1 - core) * half, half)
    part0 = pl.multiple_of(own0 + y * part, part)

    def remote(src, dst, ss, rs, d, o):
        return pltpu.make_async_remote_copy(
            src_ref=src, dst_ref=dst, send_sem=ss, recv_sem=rs, device_id=(d, o), device_id_type=MESH
        )

    def block(o):
        return pl.ds(pl.multiple_of(o * cap, cap), cap)

    def drain(ref, sem):
        pltpu.make_async_copy(ref, ref, sem).wait()

    loads = [pltpu.make_async_copy(h, v, w_sem.at[i]) for i, (h, v) in enumerate(((wg_hbm, wg), (wu_hbm, wu), (wd_hbm, wd)))]
    for c in loads:
        c.start()

    barrier = pltpu.get_barrier_semaphore()

    @pl.loop(1, n_o)
    def _(k):
        pl.semaphore_signal(barrier, inc=1, device_id=(dp, lax.rem(me + k, n_o)), device_id_type=MESH)

    @pl.loop(1, n_dp)
    def _(k):
        pl.semaphore_signal(barrier, inc=1, device_id=(lax.rem(dp + k, n_dp), me), device_id_type=MESH)

    def build(e):
        @pl.loop(0, n_o)
        def _(o):
            i = e * n_o + o
            r = rank_ref[pl.ds(i, 1), :]
            w = weight_ref[pl.ds(i, 1), :]
            m = r == lax.broadcasted_iota(jnp.int32, (cap, r.shape[1]), 0)
            at = pl.ds(pl.multiple_of(i * cap, cap), cap)
            one[at, :] = jnp.where(m, 1.0, 0.0).astype(BF16)
            scaled[at, :] = jnp.where(m, w, 0.0).astype(BF16)

        for half_, (mat, src) in enumerate(((one, tok_ref), (scaled, og_ref))):
            @pl.loop(0, rows // 256)
            def _(i, half_=half_, mat=mat, src=src):
                r0 = pl.multiple_of(i * 256, 256)
                sent[e, half_, pl.ds(r0, 256), :] = dot(mat[pl.ds(e * rows + r0, 256), :], src[...], NN).astype(BF16)

    def spread(src, dst, ss, rs, e):
        for h in range(2):
            @pl.loop(1, n_o)
            def _(k, h=h):
                to = lax.rem(me + k, n_o)
                remote(src.at[e, h, block(to)], dst.at[e, h, block(me)], ss.at[e, h], rs.at[e, h], dp, to).start()
            pltpu.make_async_copy(src.at[e, h, block(me)], dst.at[e, h, block(me)], rs.at[e, h]).start()

    def sent_all(e, ss):
        for h in range(2):
            drain(sent.at[e, h, pl.ds(0, rows - cap)], ss.at[e, h])

    def product(e, r0, store):
        @pl.loop(0, half // 192)
        def _(i):
            at = pl.ds(pl.multiple_of(r0 + i * 192, 192), 192)
            to = pl.ds(pl.multiple_of(i * 192, 192), 192)
            x = xg[e, 0, at, :]
            g = xg[e, 1, at, :]
            store[to, 0:ff] = dot(x, wg[e], NN).astype(BF16)
            store[to, ff : 2 * ff] = dot(x, wu[e], NN).astype(BF16)
            store[to, 2 * ff : 3 * ff] = dot(g, wd[e], NT).astype(BF16)

    def stage_d(e):
        for h in range(2):
            drain(xg.at[e, h], d_recv.at[e, h])
        if e == 0:
            for c in loads:
                c.wait()
        product(e, other0, mine.at[2])
        remote(mine.at[2], held.at[e % 2], h_send.at[e], h_recv.at[e], y * 2 + 1 - core, me).start()
        product(e, own0, mine.at[e % 2])

    def stage_r(e):
        cp = remote(mine.at[2], held.at[e % 2], h_send.at[e], h_recv.at[e], y * 2 + 1 - core, me)
        cp.wait_recv()
        for d in (2, 1, 3, 0):
            to = lax.rem(y + d, n_y)
            at = pl.ds(pl.multiple_of(to * part, part), part)
            own = mine.at[e % 2, at]
            own[...] = (own[...].astype(F32) + held[e % 2, at, :].astype(F32)).astype(BF16)
            if d:
                remote(own, far.at[e, d - 1], r_send.at[e, d - 1], r_recv.at[e, d - 1], to * 2 + core, me).start()
        cp.wait_send()

    def stage_a(e):
        for d in (1, 2, 3):
            drain(far.at[e, d - 1], r_recv.at[e, d - 1])
        at = pl.ds(pl.multiple_of(y * part, part), part)

        def total(c0):
            v = mine[e % 2, at, c0 : c0 + ff].astype(F32)
            for d in range(3):
                v = v + far[e, d, :, c0 : c0 + ff].astype(F32)
            return v

        gate, up, gh = total(0), total(ff), total(2 * ff)
        sig = 1.0 / (1.0 + jnp.exp(-gate))
        silu = gate * sig
        hid = (silu * up).astype(BF16)
        out = act.at[e % 3, pl.ds(part0, part)]
        out[:, 0:ff] = hid
        out[:, ff : 2 * ff] = (gh * up * sig * (1.0 + gate * (1.0 - sig))).astype(BF16)
        out[:, 2 * ff : 3 * ff] = (gh * silu).astype(BF16)
        for d in (2, 1, 3):
            remote(out, out, a_send.at[e, d - 1], a_recv.at[e, d - 1], lax.rem(y + d, n_y) * 2 + core, me).start()
        prod = (hid.astype(F32) * gh).astype(BF16)
        row = dot(jnp.ones((8, ff), BF16), prod, NT)
        dr_all[share, e : e + 1, 0:part] = row[0:1]
        for d in (1, 2, 3):
            drain(far.at[e, d - 1], r_send.at[e, d - 1])

    def stage_f(e):
        own = act.at[e % 3, pl.ds(part0, part)]
        for d in (1, 2, 3):
            drain(own, a_recv.at[e, d - 1])
            drain(own, a_send.at[e, d - 1])
        mine_ = act.at[e % 3, pl.ds(own0, half)]
        remote(mine_, mine_, c_send.at[e], c_recv.at[e], y * 2 + 1 - core, me).start()

    def stage_c(e):
        mine_ = act.at[e % 3, pl.ds(own0, half)]
        remote(mine_, mine_, c_send.at[e], c_recv.at[e], y * 2 + 1 - core, me).wait()
        sent_all(e, d_send)

        @pl.loop(0, rows // 256)
        def _(i):
            at = pl.ds(pl.multiple_of(i * 256, 256), 256)
            sent[e, 0, at, :] = dot(act[e % 3, at, 0:ff], wd[e], NN).astype(BF16)
            so = dot(act[e % 3, at, ff : 2 * ff], wg[e], NT) + dot(act[e % 3, at, 2 * ff : 3 * ff], wu[e], NT)
            sent[e, 1, at, :] = so.astype(BF16)

        spread(sent, back, t_send, t_recv, e)
        if e:
            for c in stored(e - 1):
                c.wait()

        @pl.loop(0, ff // 256)
        def _(i):
            at = pl.ds(pl.multiple_of(i * 256, 256), 256)
            st_d[at, :] = dot(act[e % 3, :, at], xg[e, 1], TN).astype(BF16)

        @pl.loop(0, xg.shape[3] // 256)
        def _(i):
            at = pl.ds(pl.multiple_of(i * 256, 256), 256)
            x = xg[e, 0, :, at]
            st_g[at, :] = dot(x, act[e % 3, :, ff : 2 * ff], TN).astype(BF16)
            st_u[at, :] = dot(x, act[e % 3, :, 2 * ff : 3 * ff], TN).astype(BF16)

        for c in stored(e):
            c.start()

    def stored(e):
        return (
            pltpu.make_async_copy(st_g, gg_hbm.at[e], o_sem.at[0]),
            pltpu.make_async_copy(st_u, gu_hbm.at[e], o_sem.at[1]),
            pltpu.make_async_copy(st_d, gd_hbm.at[e], o_sem.at[2]),
        )

    def gather(e):
        at = pl.ds(e * rows, rows)
        for h, (mat, acc) in enumerate(((scaled, acc_m), (one, acc_t))):
            drain(back.at[e, h], t_recv.at[e, h])
            v = dot(mat[at, :], back[e, h], TN)
            if e == 0:
                acc[...] = v
            else:
                acc[...] += v

    dr_all[share] = jnp.zeros(dr_all.shape[1:], F32)
    build(0)
    pl.semaphore_wait(barrier, n_o + n_dp - 2)
    spread(sent, xg, d_send, d_recv, 0)
    for e in range(1, n_e):
        build(e)
        spread(sent, xg, d_send, d_recv, e)
    stage_d(0)
    stage_r(0)
    stage_d(1)
    stage_r(1)
    stage_a(0)
    stage_d(2)
    stage_r(2)
    stage_a(1)
    stage_f(0)
    stage_c(0)
    stage_d(3)
    stage_r(3)
    stage_a(2)
    stage_f(1)
    stage_c(1)
    stage_a(3)

    @pl.loop(1, n_dp)
    def _(k):
        own = dr_all.at[share]
        remote(own, own, q_send, q_recv, lax.rem(dp + k, n_dp), me).start()

    stage_f(2)
    stage_c(2)
    stage_f(3)
    drain(dr_all.at[pl.ds(0, n_dp - 1)], q_recv)
    drain(dr_all.at[pl.ds(0, n_dp - 1)], q_send)

    @pl.loop(1, n_o)
    def _(k):
        to = lax.rem(me + k, n_o)
        remote(dr_all.at[to // 2], dr_in.at[me], v_send, v_recv, dp, to).start()

    pltpu.make_async_copy(dr_all.at[me // 2], dr_in.at[me], v_recv).start()
    stage_c(3)
    gather(0)
    gather(1)
    gather(2)
    drain(dr_in, v_recv)
    drain(dr_in.at[pl.ds(0, n_o - 1)], v_send)
    route_ref[...] = dr_in[...]
    gather(3)
    mixed_ref[...] = acc_m[...].astype(BF16)
    gtok_ref[...] = acc_t[...].astype(BF16)
    for e in range(n_e):
        sent_all(e, t_send)
    for c in stored(n_e - 1):
        c.wait()


def local(tokens, expert_ids, route_weights, w_gate, w_up, w_down, out_grad):
    tok, top = expert_ids.shape
    e_loc, width, ff = w_gate.shape
    owners = lax.axis_size("expert")
    n_dp = lax.axis_size("dp")
    experts = e_loc * owners
    cap = 3 * tok * top // (2 * experts)
    rows = owners * cap
    half, part = rows // 2, rows // n_dp
    table = jnp.arange(experts, dtype=jnp.int32)
    hit = expert_ids[:, :, None] == table
    member = jnp.any(hit, 1)
    tri = (jnp.arange(tok)[:, None] > jnp.arange(tok)[None, :]).astype(BF16)
    before = jnp.dot(tri, member.astype(BF16), preferred_element_type=F32).astype(jnp.int32)
    rank = jnp.where(member, before, -1)
    rounded = route_weights.astype(BF16).astype(F32)
    weight = jnp.sum(jnp.where(hit, rounded[:, :, None], 0.0), 1)

    def order(v):
        return v.T.reshape(owners, e_loc, tok).transpose(1, 0, 2).reshape(experts, tok)

    rank, weight = order(rank), order(weight)
    vm = pl.BlockSpec(memory_space=pltpu.VMEM)
    hbm = pl.BlockSpec(memory_space=pl.ANY)
    dma = pltpu.SemaphoreType.DMA
    mixed, gtok, route, gg, gu, gd = pl.pallas_call(
        kernel,
        out_shape=(
            jax.ShapeDtypeStruct((tok, width), BF16),
            jax.ShapeDtypeStruct((tok, width), BF16),
            jax.ShapeDtypeStruct((owners, 8, 128), F32),
            jax.ShapeDtypeStruct((e_loc, width, ff), BF16),
            jax.ShapeDtypeStruct((e_loc, width, ff), BF16),
            jax.ShapeDtypeStruct((e_loc, ff, width), BF16),
        ),
        in_specs=[vm] * 4 + [hbm] * 3,
        out_specs=[vm] * 3 + [hbm] * 3,
        scratch_shapes=[
            pltpu.VMEM((e_loc, width, ff), BF16),
            pltpu.VMEM((e_loc, width, ff), BF16),
            pltpu.VMEM((e_loc, ff, width), BF16),
            pltpu.VMEM((e_loc * rows, tok), BF16),
            pltpu.VMEM((e_loc * rows, tok), BF16),
            pltpu.VMEM((e_loc, 2, rows, width), BF16),
            pltpu.VMEM((e_loc, 2, rows, width), BF16),
            pltpu.VMEM((3, half, 3 * ff), BF16),
            pltpu.VMEM((2, half, 3 * ff), BF16),
            pltpu.VMEM((e_loc, 3, part, 3 * ff), BF16),
            pltpu.VMEM((3, rows, 3 * ff), BF16),
            pltpu.VMEM((e_loc, 2, rows, width), BF16),
            pltpu.VMEM((width, ff), BF16),
            pltpu.VMEM((width, ff), BF16),
            pltpu.VMEM((ff, width), BF16),
            pltpu.VMEM((tok, width), F32),
            pltpu.VMEM((tok, width), F32),
            pltpu.VMEM((n_dp, 8, 128), F32),
            pltpu.VMEM((owners, 8, 128), F32),
            dma((3,)), dma((3,)), dma((4, 2)), dma((4, 2)), dma((4,)), dma((4,)),
            dma((4, 3)), dma((4, 3)), dma((4, 3)), dma((4, 3)), dma((4,)), dma((4,)),
            dma((4, 2)), dma((4, 2)), dma, dma, dma, dma,
        ],
        compiler_params=pltpu.CompilerParams(
            collective_id=0, has_side_effects=True, vmem_limit_bytes=61 * 2**20
        ),
        name="moe",
    )(rank, weight, tokens, out_grad, w_gate, w_up, w_down)
    at = (lax.axis_index("expert") % 2) * cap
    per = lax.dynamic_slice_in_dim(route[:, :e_loc], at, cap, 2)
    per = per.transpose(1, 0, 2).reshape(experts, cap)
    pick = rank[:, None, :] == jnp.arange(cap, dtype=jnp.int32)[None, :, None]
    value = jnp.sum(jnp.where(pick, per[:, :, None], 0.0), 1)
    value = value.reshape(e_loc, owners, tok).transpose(1, 0, 2).reshape(experts, tok)
    grad_route = jnp.sum(jnp.where(hit, value.T[:, None, :], 0.0), 2) / rounded
    return (mixed, gtok, grad_route, gg, gu, gd)


def solution(mesh):
    tok = P("expert", "dp")
    whole = P("expert", None)
    wide = P("expert", "dp", None)
    down = P("expert", None, "dp")
    return jax.shard_map(
        local,
        mesh=mesh,
        in_specs=(tok, whole, whole, wide, wide, down, tok),
        out_specs=(tok, tok, whole, wide, wide, down),
        check_vma=False,
    )
```

time: 582 us -> 265 us (0.46); the launches traced: 573 us -> 263 us
  waiting for transfers between devices: 330 us -> 0 us
  Pallas kernels: 0 us -> 244 us
  matrix products: 55 us -> 0.19 us
  blocking collectives: 54.2 us -> 0 us
  local copies, waits for them, and re-layouts: 61.9 us -> 14.3 us
  starting transfers between devices: 34.2 us -> 0 us
  other arithmetic: 22.8 us -> 3.58 us
  between operations: 15.3 us -> 0.75 us
    pallas_call x0 -> x1, Pallas kernels: none -> 244 us  [local(): pl.pallas_call(kernel, out_shape=(jax.ShapeDtypeStruct((tok, width), BF16...]
    unnamed x3 -> x0, waiting for transfers between devices: 156 us -> none
    all_to_all x4 -> x0, waiting for transfers between devices: 99.6 us -> none  [the longest x2 69.1 us: out(): lax.all_to_all(v.reshape(layout), 'expert', split_axis=0, concat_axis=2,...]
    all_gather x1 -> x0, waiting for transfers between devices: 74 us -> none  [local(): lax.all_gather(jnp.concatenate((hid, dg, du), -1), 'dp', axis=1, tiled=True)]
    dot_general x13 -> x0, matrix products: 54.8 us -> none  [the longest x1 7.79 us: local(): jnp.einsum('erd,erf->edf', x, dg, preferred_element_type=F32).astype(BF16)]
    all_gather x2 -> x0, blocking collectives: 54.2 us -> none  [the longest x1 43 us: local(): lax.all_gather(lax.all_gather(route, 'dp', axis=1, tiled=True), 'expert',...]
    all_to_all x4 -> x0, starting transfers between devices: 33.7 us -> none  [the longest x2 17.6 us: back(): v = lax.all_to_all(v, 'expert', split_axis=1, concat_axis=0, tiled=True)]
    concatenate x2 -> x0, local copies, waits for them, and re-layouts: 25.2 us -> none  [the longest x1 22.6 us: local(): jnp.concatenate((jnp.einsum('erd,edf->erf', x, w_gate, preferred_element_...]
  transfers between devices with their start and end apart: 6 -> 0, of which waited for: 5 -> 0; matrix products, arithmetic and copies ran while one was open for 9% -> 0% of each run, Pallas kernels for 0% -> 0%
where the time goes in v2:
time: 265 us; the launch traced here: 263 us
  Pallas kernels  244 us (92%)
  local copies, waits for them, and re-layouts  14.3 us (5%)
  other arithmetic  3.58 us (1%)
    pallas_call x1, Pallas kernels, local(): pl.pallas_call(kernel, out_shape=(jax.ShapeDtypeStruct((tok, width), BF16...  244 us
    unnamed x15, local copies, waits for them, and re-layouts  11.9 us

profile of v2, /device:TPU:0, one launch (start us, length us, event | category | flops | bytes accessed | tf_op | source)
XLA Modules:
  0.0 263.1 jit_solution(5856312334653467893)
XLA Ops:
  0.6 0.7 convert_convert_fusion
  1.3 0.8 fusion.1
  2.1 0.2 fusion
  2.3 0.6 copy.23
  3.0 0.8 select_reduce_fusion.2
  3.8 0.6 copy.24
  4.4 0.0 copy-start.2
  4.4 0.0 copy-start.3
  4.4 0.0 copy-start.4
  4.4 244.3 %moe.1 = (bf16[256,512]{1,0:T(8,128)(2,1)}, bf16[256,512]{1,0:T(8,128)(2,1)}, f32[16,8,128]{2,1,0:T(8,128)}, bf16[4,512,768]{2,1,0:T(8,128)(2,1)}, bf16[4,512,76...) custom-call(s32[64,256]{1,0:T(8,128)} %bitcast.16, f32[64,256]{1,0:T(8,128)} %bitcast.18, bf16[256,512]{1,0:T(8,128)(2,1)} %tok_ref.1, ...), custom_call_target="tpu_custom_call" | custom-call | tf_op jit(solution)/shard_map/moe/pallas_call | solution.py:297
  248.8 0.8 slice.3
  249.6 0.1 dynamic-slice_bitcast_fusion
  249.7 0.0 copy-done.2
  249.7 0.7 select_reduce_fusion
  250.5 0.0 copy-done.3
  250.5 0.1 select_reduce_fusion.1
  250.6 0.0 copy-done.4
  250.6 0.6 fusion.2
  251.2 1.7 copy.32
  252.9 1.7 copy.33
  254.5 0.0 copy-start.1
  254.5 3.9 %copy.34 = bf16[4,512,768]{2,1,0:T(8,128)(2,1)} copy(bf16[4,512,768]{2,1,0:T(8,128)(2,1)} %get-tuple-element.27) | data formatting | bytes 6291456
  258.4 0.0 copy-done.1
  258.4 0.0 copy-start
  258.5 1.7 copy.35
  260.1 1.4 copy-done
  261.5 1.7 copy.36
  (5 shorter events, 0.1 us)
Async XLA Ops:
  4.4 245.3 %copy-start.2 = (s32[16,4,256]{2,0,1:T(8,128)S(1)}, s32[16,4,256]{2,0,1:T(8,128)}, u32[]{:S(2)}) copy-start(s32[16,4,256]{2,0,1:T(8,128)} %copy.23) | copy-start | bytes 196612
  4.4 246.1 %copy-start.3 = (s32[256,8]{0,1:T(8,128)S(1)}, s32[256,8]{0,1:T(8,128)}, u32[]{:S(2)}) copy-start(s32[256,8]{0,1:T(8,128)} %param.8) | copy-start | bytes 24580
  4.4 246.2 %copy-start.4 = (f32[256,8]{0,1:T(8,128)S(1)}, f32[256,8]{0,1:T(8,128)}, u32[]{:S(2)}) copy-start(f32[256,8]{0,1:T(8,128)} %param.9) | copy-start | bytes 24580
  254.5 3.9 %copy-start.1 = (bf16[4,512,768]{2,1,0:T(8,128)(2,1)S(1)}, bf16[4,512,768]{2,1,0:T(8,128)(2,1)}, u32[]{:S(2)}) copy-start(bf16[4,512,768]{2,1,0:T(8,128)(2,1)} %get-tuple-element.28) | copy-start | bytes 9437188
  258.4 3.0 %copy-start = (bf16[4,768,512]{2,1,0:T(8,128)(2,1)S(1)}, bf16[4,768,512]{2,1,0:T(8,128)(2,1)}, u32[]{:S(2)}) copy-start(bf16[4,768,512]{2,1,0:T(8,128)(2,1)} %get-tuple-element.29) | copy-start | bytes 9437188

commit v3 on v2

--- a/solution.py
+++ b/solution.py
@@ -116,26 +116,55 @@
         remote(mine.at[2], held.at[e % 2], h_send.at[e], h_recv.at[e], y * 2 + 1 - core, me).start()
         product(e, own0, mine.at[e % 2])
 
+    left, right = lax.rem(y + n_y - 1, n_y), lax.rem(y + 1, n_y)
+    across = lax.rem(y + 2, n_y)
+    hp = part // 2
+
+    def piece(y_, h):
+        return pl.ds(pl.multiple_of(y_ * part + h * hp, hp), hp)
+
+    def hop(e, i):
+        to, y_, h, dst = (
+            (left, across, 0, (2, 0)), (right, across, 1, (2, 1)),
+            (left, left, 1, (0, 1)), (right, right, 0, (1, 0)),
+            (left, left, 0, (0, 0)), (right, right, 1, (1, 1)),
+        )[i]
+        return remote(
+            mine.at[e % 2, piece(y_, h)], far.at[e, dst[0], pl.ds(dst[1] * hp, hp)],
+            r_send.at[e, i], r_recv.at[e, i], to * 2 + core, me,
+        )
+
     def stage_r(e):
         cp = remote(mine.at[2], held.at[e % 2], h_send.at[e], h_recv.at[e], y * 2 + 1 - core, me)
         cp.wait_recv()
-        for d in (2, 1, 3, 0):
-            to = lax.rem(y + d, n_y)
-            at = pl.ds(pl.multiple_of(to * part, part), part)
+        for y_, go in ((across, (0, 1)), (left, (2,)), (right, (3,)), (y, ())):
+            at = pl.ds(pl.multiple_of(y_ * part, part), part)
             own = mine.at[e % 2, at]
             own[...] = (own[...].astype(F32) + held[e % 2, at, :].astype(F32)).astype(BF16)
-            if d:
-                remote(own, far.at[e, d - 1], r_send.at[e, d - 1], r_recv.at[e, d - 1], to * 2 + core, me).start()
+            for i in go:
+                hop(e, i).start()
         cp.wait_send()
 
+    def stage_p(e):
+        for i, y_, h in ((0, left, 0), (1, right, 1)):
+            hop(e, i).wait_recv()
+            own = mine.at[e % 2, piece(y_, h)]
+            own[...] = (own[...].astype(F32) + far[e, 2, h * hp : (h + 1) * hp, :].astype(F32)).astype(BF16)
+            hop(e, i + 4).start()
+
+    def relay(e, i):
+        y_, r0, n, to = ((y, 0, part, right), (y, 0, part, left), (left, 0, hp, right), (right, hp, hp, left))[i]
+        at = act.at[e % 3, pl.ds(pl.multiple_of(own0 + y_ * part + r0, hp), n)]
+        return remote(at, at, a_send.at[e, i], a_recv.at[e, i], to * 2 + core, me)
+
     def stage_a(e):
-        for d in (1, 2, 3):
-            drain(far.at[e, d - 1], r_recv.at[e, d - 1])
+        for i in range(2, 6):
+            hop(e, i).wait_recv()
         at = pl.ds(pl.multiple_of(y * part, part), part)
 
         def total(c0):
             v = mine[e % 2, at, c0 : c0 + ff].astype(F32)
-            for d in range(3):
+            for d in range(2):
                 v = v + far[e, d, :, c0 : c0 + ff].astype(F32)
             return v
 
@@ -147,19 +176,24 @@
         out[:, 0:ff] = hid
         out[:, ff : 2 * ff] = (gh * up * sig * (1.0 + gate * (1.0 - sig))).astype(BF16)
         out[:, 2 * ff : 3 * ff] = (gh * silu).astype(BF16)
-        for d in (2, 1, 3):
-            remote(out, out, a_send.at[e, d - 1], a_recv.at[e, d - 1], lax.rem(y + d, n_y) * 2 + core, me).start()
+        relay(e, 0).start()
+        relay(e, 1).start()
         prod = (hid.astype(F32) * gh).astype(BF16)
         row = dot(jnp.ones((8, ff), BF16), prod, NT)
         dr_all[share, e : e + 1, 0:part] = row[0:1]
-        for d in (1, 2, 3):
-            drain(far.at[e, d - 1], r_send.at[e, d - 1])
+        for i in range(6):
+            hop(e, i).wait_send()
+
+    def stage_g(e):
+        for i in range(2):
+            relay(e, i).wait_recv()
+            relay(e, i + 2).start()
 
     def stage_f(e):
-        own = act.at[e % 3, pl.ds(part0, part)]
-        for d in (1, 2, 3):
-            drain(own, a_recv.at[e, d - 1])
-            drain(own, a_send.at[e, d - 1])
+        for i in (2, 3):
+            relay(e, i).wait_recv()
+        for i in range(4):
+            relay(e, i).wait_send()
         mine_ = act.at[e % 3, pl.ds(own0, half)]
         remote(mine_, mine_, c_send.at[e], c_recv.at[e], y * 2 + 1 - core, me).start()
 
@@ -176,6 +210,8 @@
             sent[e, 1, at, :] = so.astype(BF16)
 
         spread(sent, back, t_send, t_recv, e)
+
+    def stage_w(e):
         if e:
             for c in stored(e - 1):
                 c.wait()
@@ -219,30 +255,28 @@
     for e in range(1, n_e):
         build(e)
         spread(sent, xg, d_send, d_recv, e)
-    stage_d(0)
-    stage_r(0)
-    stage_d(1)
-    stage_r(1)
-    stage_a(0)
-    stage_d(2)
-    stage_r(2)
-    stage_a(1)
-    stage_f(0)
-    stage_c(0)
-    stage_d(3)
-    stage_r(3)
-    stage_a(2)
-    stage_f(1)
-    stage_c(1)
-    stage_a(3)
+    for e in range(n_e):
+        stage_d(e)
+        stage_r(e)
+        if e == 0:
+            stage_p(0)
+            stage_a(0)
+            continue
+        if e > 1:
+            stage_w(e - 2)
+        stage_g(e - 1)
+        stage_p(e)
+        stage_f(e - 1)
+        stage_c(e - 1)
+        stage_a(e)
 
     @pl.loop(1, n_dp)
     def _(k):
         own = dr_all.at[share]
         remote(own, own, q_send, q_recv, lax.rem(dp + k, n_dp), me).start()
 
-    stage_f(2)
-    stage_c(2)
+    stage_g(3)
+    stage_w(2)
     stage_f(3)
     drain(dr_all.at[pl.ds(0, n_dp - 1)], q_recv)
     drain(dr_all.at[pl.ds(0, n_dp - 1)], q_send)
@@ -254,6 +288,7 @@
 
     pltpu.make_async_copy(dr_all.at[me // 2], dr_in.at[me], v_recv).start()
     stage_c(3)
+    stage_w(3)
     gather(0)
     gather(1)
     gather(2)
@@ -267,6 +302,23 @@
         sent_all(e, t_send)
     for c in stored(n_e - 1):
         c.wait()
+
+
+def pass_on(*refs):
+    n = (len(refs) - 2) // 3
+    sems_in, sems_out = refs[-2:]
+    arrive, leave = [], []
+    for i, (a, b, v) in enumerate(zip(refs[:n], refs[n : 2 * n], refs[2 * n : 3 * n])):
+        for p in range(a.shape[0]):
+            arrive.append(pltpu.make_async_copy(a.at[p], v.at[p], sems_in.at[i, p]))
+            leave.append(pltpu.make_async_copy(v.at[p], b.at[p], sems_out.at[i, p]))
+    for c in arrive:
+        c.start()
+    for c, d in zip(arrive, leave):
+        c.wait()
+        d.start()
+    for d in leave:
+        d.wait()
 
 
 def local(tokens, expert_ids, route_weights, w_gate, w_up, w_down, out_grad):
@@ -327,7 +379,7 @@
             pltpu.VMEM((n_dp, 8, 128), F32),
             pltpu.VMEM((owners, 8, 128), F32),
             dma((3,)), dma((3,)), dma((4, 2)), dma((4, 2)), dma((4,)), dma((4,)),
-            dma((4, 3)), dma((4, 3)), dma((4, 3)), dma((4, 3)), dma((4,)), dma((4,)),
+            dma((4, 6)), dma((4, 6)), dma((4, 4)), dma((4, 4)), dma((4,)), dma((4,)),
             dma((4, 2)), dma((4, 2)), dma, dma, dma, dma,
         ],
         compiler_params=pltpu.CompilerParams(
@@ -335,6 +387,16 @@
         ),
         name="moe",
     )(rank, weight, tokens, out_grad, w_gate, w_up, w_down)
+    results = (gg, gu, gd)
+    gg, gu, gd = pl.pallas_call(
+        pass_on,
+        out_shape=tuple(jax.ShapeDtypeStruct(v.shape, v.dtype) for v in results),
+        in_specs=[hbm] * 3,
+        out_specs=[hbm] * 3,
+        scratch_shapes=[pltpu.VMEM(v.shape, v.dtype) for v in results] + [dma((3, e_loc)), dma((3, e_loc))],
+        compiler_params=pltpu.CompilerParams(vmem_limit_bytes=60 * 2**20),
+        name="pass_on",
+    )(*results)
     at = (lax.axis_index("expert") % 2) * cap
     per = lax.dynamic_slice_in_dim(route[:, :e_loc], at, cap, 2)
     per = per.transpose(1, 0, 2).reshape(experts, cap)

time: 265 us -> 242 us (0.913)
  Pallas kernels: 244 us -> 231 us
  local copies, waits for them, and re-layouts: 14.3 us -> 3.76 us
    pallas_call x1, Pallas kernels: 244 us -> 223 us  [local(): pl.pallas_call(kernel, out_shape=(jax.ShapeDtypeStruct((tok, width), BF16...]
    unnamed x15 -> x12, local copies, waits for them, and re-layouts: 11.9 us -> 1.43 us
    pallas_call x0 -> x1, Pallas kernels: none -> 7.35 us  [local(): pl.pallas_call(pass_on, out_shape=tuple((jax.ShapeDtypeStruct(v.shape, v....]
where the time goes in v3:
time: 242 us; the launch traced here: 239 us
  Pallas kernels  231 us (95%)
  local copies, waits for them, and re-layouts  3.76 us (2%)
  other arithmetic  3.58 us (1%)
    pallas_call x1, Pallas kernels, local(): pl.pallas_call(kernel, out_shape=(jax.ShapeDtypeStruct((tok, width), BF16...  223 us
    pallas_call x1, Pallas kernels, local(): pl.pallas_call(pass_on, out_shape=tuple((jax.ShapeDtypeStruct(v.shape, v....  7.35 us

profile of v3, /device:TPU:0, one launch (start us, length us, event | category | flops | bytes accessed | tf_op | source)
XLA Modules:
  0.0 239.0 jit_solution(12679098950244739440)
XLA Ops:
  0.6 0.7 convert_convert_fusion
  1.3 0.8 fusion.1
  2.1 0.2 fusion
  2.3 0.6 copy.23
  3.0 0.8 select_reduce_fusion.2
  3.8 0.6 copy.24
  4.4 0.0 copy-start
  4.4 0.0 copy-start.3
  4.4 0.0 copy-start.4
  4.4 223.3 %moe.1 = (bf16[256,512]{1,0:T(8,128)(2,1)}, bf16[256,512]{1,0:T(8,128)(2,1)}, f32[16,8,128]{2,1,0:T(8,128)}, bf16[4,512,768]{2,1,0:T(8,128)(2,1)}, bf16[4,512,76...) custom-call(s32[64,256]{1,0:T(8,128)} %bitcast.16, f32[64,256]{1,0:T(8,128)} %bitcast.18, bf16[256,512]{1,0:T(8,128)(2,1)} %tok_ref.1, ...), custom_call_target="tpu_custom_call" | custom-call | tf_op jit(solution)/shard_map/moe/pallas_call | solution.py:349
  227.8 0.8 slice.3
  228.6 0.1 dynamic-slice_bitcast_fusion
  228.7 0.0 copy-done
  228.7 0.7 select_reduce_fusion
  229.5 0.0 copy-done.3
  229.5 0.1 select_reduce_fusion.1
  229.6 0.0 copy-done.4
  229.6 0.6 fusion.2
  230.2 0.0 copy-start.2
  230.2 0.0 copy-start.1
  230.2 7.3 %pass_on.1 = (bf16[4,512,768]{2,1,0:T(8,128)(2,1)}, bf16[4,512,768]{2,1,0:T(8,128)(2,1)}, bf16[4,768,512]{2,1,0:T(8,128)(2,1)}) custom-call(bf16[4,512,768]{2,1,0:T(8,128)(2,1)} %get-tuple-element.18.refs_0_, bf16[4,512,768]{2,1,0:T(8,128)(2,1)} %get-tuple-element.19.refs_1_, bf16[4,768,512]{2,1,0:T(8,128)(2,1)} %get-tuple-element.20.refs_2_), custom_call_target="tpu_custom_call" | custom-call | tf_op jit(solution)/shard_map/pass_on/pallas_call | solution.py:391
  237.6 0.0 copy-done.2
  237.6 0.7 copy.29
  238.3 0.0 copy-done.1
  238.3 0.7 copy.30
  (5 shorter events, 0.1 us)
Async XLA Ops:
  4.4 224.3 %copy-start = (s32[16,4,256]{2,0,1:T(8,128)S(1)}, s32[16,4,256]{2,0,1:T(8,128)}, u32[]{:S(2)}) copy-start(s32[16,4,256]{2,0,1:T(8,128)} %copy.23) | copy-start | bytes 196612
  4.4 225.1 %copy-start.3 = (s32[256,8]{0,1:T(8,128)S(1)}, s32[256,8]{0,1:T(8,128)}, u32[]{:S(2)}) copy-start(s32[256,8]{0,1:T(8,128)} %param.8) | copy-start | bytes 24580
  4.4 225.2 %copy-start.4 = (f32[256,8]{0,1:T(8,128)S(1)}, f32[256,8]{0,1:T(8,128)}, u32[]{:S(2)}) copy-start(f32[256,8]{0,1:T(8,128)} %param.9) | copy-start | bytes 24580
  230.2 7.4 %copy-start.2 = (bf16[256,512]{1,0:T(8,128)(2,1)S(1)}, bf16[256,512]{1,0:T(8,128)(2,1)}, u32[]{:S(2)}) copy-start(bf16[256,512]{1,0:T(8,128)(2,1)} %get-tuple-element.30) | copy-start | bytes 786436
  230.2 8.1 %copy-start.1 = (bf16[256,512]{1,0:T(8,128)(2,1)S(1)}, bf16[256,512]{1,0:T(8,128)(2,1)}, u32[]{:S(2)}) copy-start(bf16[256,512]{1,0:T(8,128)(2,1)} %get-tuple-element.31) | copy-start | bytes 786436

commit v4 on v3

--- a/solution.py
+++ b/solution.py
@@ -83,11 +83,12 @@
                 r0 = pl.multiple_of(i * 256, 256)
                 sent[e, half_, pl.ds(r0, 256), :] = dot(mat[pl.ds(e * rows + r0, 256), :], src[...], NN).astype(BF16)
 
-    def spread(src, dst, ss, rs, e):
-        for h in range(2):
-            @pl.loop(1, n_o)
-            def _(k, h=h):
-                to = lax.rem(me + k, n_o)
+    ex, ez = me // 4, me % 4
+    peers = [lax.rem(ex + dx, 4) * 4 + lax.rem(ez + dz, 4) for dx, dz in ((2, 2), (0, 1), (2, 1), (3, 0), (1, 2), (0, 3), (2, 3), (1, 0), (3, 2), (1, 1), (2, 0), (3, 3), (0, 2), (1, 3), (3, 1))]
+
+    def spread(src, dst, ss, rs, e, hs=(0, 1)):
+        for h in hs:
+            for to in peers:
                 remote(src.at[e, h, block(to)], dst.at[e, h, block(me)], ss.at[e, h], rs.at[e, h], dp, to).start()
             pltpu.make_async_copy(src.at[e, h, block(me)], dst.at[e, h, block(me)], rs.at[e, h]).start()
 
@@ -206,10 +207,16 @@
         def _(i):
             at = pl.ds(pl.multiple_of(i * 256, 256), 256)
             sent[e, 0, at, :] = dot(act[e % 3, at, 0:ff], wd[e], NN).astype(BF16)
+
+        spread(sent, back, t_send, t_recv, e, (0,))
+
+        @pl.loop(0, rows // 256)
+        def _(i):
+            at = pl.ds(pl.multiple_of(i * 256, 256), 256)
             so = dot(act[e % 3, at, ff : 2 * ff], wg[e], NT) + dot(act[e % 3, at, 2 * ff : 3 * ff], wu[e], NT)
             sent[e, 1, at, :] = so.astype(BF16)
 
-        spread(sent, back, t_send, t_recv, e)
+        spread(sent, back, t_send, t_recv, e, (1,))
 
     def stage_w(e):
         if e:
@@ -252,11 +259,14 @@
     build(0)
     pl.semaphore_wait(barrier, n_o + n_dp - 2)
     spread(sent, xg, d_send, d_recv, 0)
-    for e in range(1, n_e):
-        build(e)
-        spread(sent, xg, d_send, d_recv, e)
+    build(1)
+    spread(sent, xg, d_send, d_recv, 1)
+    build(2)
+    build(3)
     for e in range(n_e):
         stage_d(e)
+        if e + 2 < n_e:
+            spread(sent, xg, d_send, d_recv, e + 2)
         stage_r(e)
         if e == 0:
             stage_p(0)

time: 242 us -> 214 us (0.88)
  Pallas kernels: 231 us -> 204 us
    pallas_call x1, Pallas kernels: 223 us -> 197 us  [local(): pl.pallas_call(kernel, out_shape=(jax.ShapeDtypeStruct((tok, width), BF16...]
where the time goes in v4:
time: 214 us; the launch traced here: 213 us
  Pallas kernels  204 us (95%)
  local copies, waits for them, and re-layouts  3.76 us (2%)
  other arithmetic  3.58 us (2%)
    pallas_call x1, Pallas kernels, local(): pl.pallas_call(kernel, out_shape=(jax.ShapeDtypeStruct((tok, width), BF16...  197 us
    pallas_call x1, Pallas kernels, local(): pl.pallas_call(pass_on, out_shape=tuple((jax.ShapeDtypeStruct(v.shape, v....  7.35 us

profile of v4, /device:TPU:0, one launch (start us, length us, event | category | flops | bytes accessed | tf_op | source)
XLA Modules:
  0.0 212.7 jit_solution(9574535491684543396)
XLA Ops:
  0.6 0.7 convert_convert_fusion
  1.3 0.8 fusion.1
  2.1 0.2 fusion
  2.3 0.6 copy.23
  3.0 0.8 select_reduce_fusion.2
  3.8 0.6 copy.24
  4.4 0.0 copy-start
  4.4 0.0 copy-start.3
  4.4 0.0 copy-start.4
  4.4 197.1 %moe.1 = (bf16[256,512]{1,0:T(8,128)(2,1)}, bf16[256,512]{1,0:T(8,128)(2,1)}, f32[16,8,128]{2,1,0:T(8,128)}, bf16[4,512,768]{2,1,0:T(8,128)(2,1)}, bf16[4,512,76...) custom-call(s32[64,256]{1,0:T(8,128)} %bitcast.16, f32[64,256]{1,0:T(8,128)} %bitcast.18, bf16[256,512]{1,0:T(8,128)(2,1)} %tok_ref.1, ...), custom_call_target="tpu_custom_call" | custom-call | tf_op jit(solution)/shard_map/moe/pallas_call | solution.py:359
  201.5 0.8 slice.3
  202.4 0.1 dynamic-slice_bitcast_fusion
  202.5 0.0 copy-done
  202.5 0.7 select_reduce_fusion
  203.2 0.0 copy-done.3
  203.2 0.1 select_reduce_fusion.1
  203.3 0.0 copy-done.4
  203.3 0.6 fusion.2
  203.9 0.0 copy-start.2
  203.9 0.0 copy-start.1
  203.9 7.3 %pass_on.1 = (bf16[4,512,768]{2,1,0:T(8,128)(2,1)}, bf16[4,512,768]{2,1,0:T(8,128)(2,1)}, bf16[4,768,512]{2,1,0:T(8,128)(2,1)}) custom-call(bf16[4,512,768]{2,1,0:T(8,128)(2,1)} %get-tuple-element.18.refs_0_, bf16[4,512,768]{2,1,0:T(8,128)(2,1)} %get-tuple-element.19.refs_1_, bf16[4,768,512]{2,1,0:T(8,128)(2,1)} %get-tuple-element.20.refs_2_), custom_call_target="tpu_custom_call" | custom-call | tf_op jit(solution)/shard_map/pass_on/pallas_call | solution.py:401
  211.3 0.0 copy-done.2
  211.3 0.7 copy.29
  212.0 0.0 copy-done.1
  212.0 0.7 copy.30
  (5 shorter events, 0.1 us)
Async XLA Ops:
  4.4 198.0 %copy-start = (s32[16,4,256]{2,0,1:T(8,128)S(1)}, s32[16,4,256]{2,0,1:T(8,128)}, u32[]{:S(2)}) copy-start(s32[16,4,256]{2,0,1:T(8,128)} %copy.23) | copy-start | bytes 196612
  4.4 198.8 %copy-start.3 = (s32[256,8]{0,1:T(8,128)S(1)}, s32[256,8]{0,1:T(8,128)}, u32[]{:S(2)}) copy-start(s32[256,8]{0,1:T(8,128)} %param.8) | copy-start | bytes 24580
  4.4 198.9 %copy-start.4 = (f32[256,8]{0,1:T(8,128)S(1)}, f32[256,8]{0,1:T(8,128)}, u32[]{:S(2)}) copy-start(f32[256,8]{0,1:T(8,128)} %param.9) | copy-start | bytes 24580
  203.9 7.4 %copy-start.2 = (bf16[256,512]{1,0:T(8,128)(2,1)S(1)}, bf16[256,512]{1,0:T(8,128)(2,1)}, u32[]{:S(2)}) copy-start(bf16[256,512]{1,0:T(8,128)(2,1)} %get-tuple-element.30) | copy-start | bytes 786436
  203.9 8.1 %copy-start.1 = (bf16[256,512]{1,0:T(8,128)(2,1)S(1)}, bf16[256,512]{1,0:T(8,128)(2,1)}, u32[]{:S(2)}) copy-start(bf16[256,512]{1,0:T(8,128)(2,1)} %get-tuple-element.31) | copy-start | bytes 786436
